TPU v7x, 128 devices: a whole 4x4x4 slice. The times are simulated.
128 devices in a mesh: dp: 4 (over z_hi, core), seq: 32 (over x, z_lo, y).
Axes of the slice: x: 4, y: 4, z: 4 (z_hi: 2, z_lo: 2; z = z_hi * 2 + z_lo), core: 2. Of those that a mesh axis runs over, the one named last changes fastest.
Arguments:
- block_input: bfloat16 [4, 32, 256, 1152], P('dp', 'seq'), may hold values from -45 to 45
- out_grad: bfloat16 [4, 32, 256, 1152], P('dp', 'seq'), may hold values from -6 to 6
- spatial_keep: int32 [4, 32, 256, 1152], P('dp', 'seq'), may hold values 0 or 1
- temporal_keep: int32 [4, 32, 256, 1152], P('dp', None, 'seq'), may hold values 0 or 1
- spatial_qkv: bfloat16 [1152, 1728], replicated, may hold values from -0.1875 to 0.1875
- spatial_out: bfloat16 [1152, 576], replicated, may hold values from -0.25 to 0.25
- temporal_qkv: bfloat16 [1152, 1728], replicated, may hold values from -0.1875 to 0.1875
- temporal_out: bfloat16 [1152, 576], replicated, may hold values from -0.25 to 0.25
Outputs:
- input_grad: bfloat16 [4, 32, 256, 1152], P('dp', 'seq')
- spatial_qkv_grad: float32 [1152, 1728], P('seq', 'dp')
- spatial_out_grad: float32 [1152, 576], P('seq', 'dp')
- temporal_qkv_grad: float32 [1152, 1728], P('seq', 'dp')
- temporal_out_grad: float32 [1152, 576], P('seq', 'dp')
All inputs are finite; a program needn't handle non-finite values. No bound on the sum of `spatial_keep` or of `temporal_keep` on one device may be relied on, other than what follows from the above.
Results may differ from a plain program's by a relative error of at most 0.03.
Values may be sent and summed in bfloat16 or wider, within the bound.
A program may use at most 128 MiB of HBM per device.

v0:
```python
import jax
import jax.numpy as jnp
from jax import lax
from jax.sharding import PartitionSpec as P

H = 8
HD = 72


def section_forward(tokens, w_qkv, w_out, keep):
    groups, length, extra, width = tokens.shape
    inner = w_out.shape[1]
    scale = HD ** (-0.5)
    zf = tokens.astype(jnp.float32)
    inv = lax.rsqrt(jnp.mean(zf * zf, axis=-1, keepdims=True) + 1e-06)
    normed = (zf * inv).astype(jnp.bfloat16)
    qkv = jnp.dot(normed.reshape(-1, width), w_qkv, preferred_element_type=jnp.float32).astype(
        jnp.bfloat16
    )
    qkv = qkv.reshape(groups, length, extra, 3, H, HD)
    query = qkv[:, :, :, 0]
    keys = qkv[:, :, :, 1]
    values = qkv[:, :, :, 2]
    scores = (
        jnp.einsum("aiehc,ajehc->aehij", query, keys, preferred_element_type=jnp.float32) * scale
    )
    expo = jnp.exp(scores)
    probs = expo / jnp.sum(expo, axis=-1, keepdims=True)
    probs_low = probs.astype(jnp.bfloat16)
    mixed = jnp.einsum("aehij,ajehc->aiehc", probs_low, values, preferred_element_type=jnp.float32)
    mixed = mixed.astype(jnp.bfloat16).reshape(-1, inner)
    proj = lax.dot_general(
        mixed, w_out, (((1,), (1,)), ((), ())), preferred_element_type=jnp.float32
    )
    proj = proj.reshape(groups, length, extra, width)
    keepf = keep.astype(jnp.float32) / 0.9
    output = (zf + proj * keepf).astype(jnp.bfloat16)
    return (output, (zf, inv, normed, query, keys, values, probs, probs_low, mixed, keepf))


def section_backward(grad, saved, w_qkv, w_out):
    zf, inv, normed, query, keys, values, probs, probs_low, mixed, keepf = saved
    groups, length, extra, width = zf.shape
    inner = w_out.shape[1]
    scale = HD ** (-0.5)
    dyf = grad.astype(jnp.float32)
    d_proj = (dyf * keepf).astype(jnp.bfloat16).reshape(-1, width)
    g_out = lax.dot_general(
        d_proj, mixed, (((0,), (0,)), ((), ())), preferred_element_type=jnp.float32
    )
    d_mixed = jnp.dot(d_proj, w_out, preferred_element_type=jnp.float32).astype(jnp.bfloat16)
    d_mixed = d_mixed.reshape(groups, length, extra, H, HD)
    d_probs = jnp.einsum("aiehc,ajehc->aehij", d_mixed, values, preferred_element_type=jnp.float32)
    d_scores = probs * (d_probs - jnp.sum(probs * d_probs, axis=-1, keepdims=True)) * scale
    d_scores = d_scores.astype(jnp.bfloat16)
    d_query = jnp.einsum("aehij,ajehc->aiehc", d_scores, keys, preferred_element_type=jnp.float32)
    d_keys = jnp.einsum("aehij,aiehc->ajehc", d_scores, query, preferred_element_type=jnp.float32)
    d_values = jnp.einsum(
        "aehij,aiehc->ajehc", probs_low, d_mixed, preferred_element_type=jnp.float32
    )
    d_qkv = (
        jnp.stack([d_query, d_keys, d_values], axis=3).astype(jnp.bfloat16).reshape(-1, 3 * inner)
    )
    g_qkv = lax.dot_general(
        normed.reshape(-1, width),
        d_qkv,
        (((0,), (0,)), ((), ())),
        preferred_element_type=jnp.float32,
    )
    d_normed = lax.dot_general(
        d_qkv, w_qkv, (((1,), (1,)), ((), ())), preferred_element_type=jnp.float32
    )
    d_normed = d_normed.reshape(groups, length, extra, width)
    centered = zf * inv
    d_input = dyf + inv * (
        d_normed - centered * jnp.mean(d_normed * centered, axis=-1, keepdims=True)
    )
    return (d_input, g_qkv, g_out)


def shards(
    block_input,
    out_grad,
    spatial_keep,
    temporal_keep,
    spatial_qkv,
    spatial_out,
    temporal_qkv,
    temporal_out,
):
    clips, frame_rows, positions, width = block_input.shape
    grad_by_pos = lax.all_to_all(out_grad, "seq", split_axis=2, concat_axis=1, tiled=True)
    first, saved_space = section_forward(
        block_input.reshape(clips * frame_rows, positions, 1, width),
        spatial_qkv,
        spatial_out,
        spatial_keep.reshape(clips * frame_rows, positions, 1, width),
    )
    first = first.reshape(clips, frame_rows, positions, width)
    first_by_pos = lax.all_to_all(first, "seq", split_axis=2, concat_axis=1, tiled=True)
    unused, saved_time = section_forward(first_by_pos, temporal_qkv, temporal_out, temporal_keep)
    d_first, g_qkv_time, g_out_time = section_backward(
        grad_by_pos, saved_time, temporal_qkv, temporal_out
    )
    d_first = lax.all_to_all(
        d_first.astype(jnp.bfloat16), "seq", split_axis=1, concat_axis=2, tiled=True
    )
    d_input, g_qkv_space, g_out_space = section_backward(
        d_first.reshape(clips * frame_rows, positions, 1, width),
        saved_space,
        spatial_qkv,
        spatial_out,
    )
    input_grad = d_input.reshape(clips, frame_rows, positions, width).astype(jnp.bfloat16)
    grads = (g_qkv_space, g_out_space, g_qkv_time, g_out_time)
    summed = (
        lax.psum_scatter(
            grads[0].astype(jnp.bfloat16), "seq", scatter_dimension=0, tiled=True
        ).astype(jnp.float32),
        lax.psum_scatter(
            grads[1].astype(jnp.bfloat16), "seq", scatter_dimension=0, tiled=True
        ).astype(jnp.float32),
        lax.psum_scatter(
            grads[2].astype(jnp.bfloat16), "seq", scatter_dimension=0, tiled=True
        ).astype(jnp.float32),
        lax.psum_scatter(
            grads[3].astype(jnp.bfloat16), "seq", scatter_dimension=0, tiled=True
        ).astype(jnp.float32),
    )
    summed = (
        lax.psum_scatter(
            summed[0].astype(jnp.bfloat16), "dp", scatter_dimension=1, tiled=True
        ).astype(jnp.float32),
        lax.psum_scatter(
            summed[1].astype(jnp.bfloat16), "dp", scatter_dimension=1, tiled=True
        ).astype(jnp.float32),
        lax.psum_scatter(
            summed[2].astype(jnp.bfloat16), "dp", scatter_dimension=1, tiled=True
        ).astype(jnp.float32),
        lax.psum_scatter(
            summed[3].astype(jnp.bfloat16), "dp", scatter_dimension=1, tiled=True
        ).astype(jnp.float32),
    )
    return (input_grad, summed[0], summed[1], summed[2], summed[3])


def solution(mesh):
    return jax.shard_map(
        shards,
        mesh=mesh,
        in_specs=(
            P("dp", "seq", None, None),
            P("dp", "seq", None, None),
            P("dp", "seq", None, None),
            P("dp", None, "seq", None),
            P(),
            P(),
            P(),
            P(),
        ),
        out_specs=(
            P("dp", "seq", None, None),
            P("seq", "dp"),
            P("seq", "dp"),
            P("seq", "dp"),
            P("seq", "dp"),
        ),
        check_vma=False,
    )
```

profile of v0, /device:TPU:0, one launch (start us, length us, event | category | flops | bytes accessed | tf_op | source)
XLA Modules:
  0.0 507.7 jit_solution(7987657167091826975)
XLA Ops:
  7.2 2.1 copy.106
  9.8 5.0 reduce.16
  14.8 2.6 reshape.622
  17.4 9.2 %all-to-all-start = ((bf16[32,2,4608]{2,1,0:T(2,128)(2,1)}), bf16[32,2,4608]{2,1,0:T(2,128)(2,1)}, u32[]{:S(2)}, u32[]{:S(2)}) async-start(bf16[32,2,4608]{2,1,0:T(2,128)(2,1)} %reshape.622), calls=%async_computation | async-start | bytes 1179648 | tf_op jit(solution)/shard_map/all_to_all | solution.py:92
  26.9 3.6 convolution_convert_fusion.5
  33.8 1.9 copy.105
  35.8 6.0 %reduce.15 = bf16[256,1152]{1,0:T(8,128)(2,1)} reduce(bf16[256,1,1,1152]{3,2,1,0:T(2,128)(2,1)} %bitcast.234, bf16[]{:T(256)} %broadcast.196), dimensions={1,2}, to_apply=%bitcast.230.reduce_sub_computation | reduce | bytes 1179650
  41.7 2.5 reshape.620
  44.3 9.1 %all-to-all-start.1 = ((bf16[32,2,4608]{2,1,0:T(2,128)(2,1)}), bf16[32,2,4608]{2,1,0:T(2,128)(2,1)}, u32[]{:S(2)}, u32[]{:S(2)}) async-start(bf16[32,2,4608]{2,1,0:T(2,128)(2,1)} %reshape.620), calls=%async_computation.1 | async-start | bytes 1179648 | tf_op jit(solution)/shard_map/all_to_all | solution.py:100
  53.4 4.7 reshape.623
  58.1 2.6 convert.6
  67.1 4.6 reshape.621
  71.7 2.2 fusion.47
  74.0 4.7 convolution_convert_fusion.4
  78.7 2.2 copy.43
  80.9 4.0 reshape.593
  84.9 2.7 fusion.114
  87.6 3.1 fusion.85
  90.7 2.7 convolution_bitcast_fusion
  96.5 3.9 convolution_bitcast_fusion.2
  100.4 3.9 convolution_bitcast_fusion.1
  104.3 2.0 copy.61
  111.4 3.6 convert_element_type.349
  115.0 4.9 fusion.52
  120.0 2.9 fusion.58
  123.0 8.5 %all-to-all-start.2 = ((bf16[1,32,8,1152]{3,2,0,1:T(8,128)(2,1)}), bf16[1,32,8,1152]{3,2,0,1:T(8,128)(2,1)}, u32[]{:S(2)}, u32[]{:S(2)}) async-start(bf16[1,32,8,1152]{3,2,0,1:T(8,128)(2,1)} %fusion.58), calls=%async_computation.2 | async-start | bytes 1179648 | tf_op jit(solution)/shard_map/all_to_all | solution.py:105
  131.8 3.0 convolution_convert_fusion.2
  134.8 3.3 convolution_convert_fusion
  138.1 4.6 all-to-all-done.2
  145.7 1.8 fusion.95
  147.5 4.5 fusion.31
  152.1 5.3 %fusion.34 = bf16[1,256,1,1,8,72]{1,5,4,3,2,0:T(8,128)(2,1)} fusion(f32[8,256,256]{1,2,0:T(8,128)} %fusion.95, bf16[1,256,1,3,8,72]{1,5,4,3,2,0:T(8,128)(2,1)S(1)} %bitcast.248, f32[8,256,256]{1,2,0:T(8,128)} %copy-done.11, f32[8,256]{1,0:T(8,128)S(1)} %get-tuple-element.18), kind=kOutput, calls=%fused_computation.48 | convolution fusion | flops 80218368 | bytes 8994816 | tf_op jit(solution)/shard_map/aehij,aiehc->ajehc/dot_general | solution.py:57
  158.5 3.4 convolution_convert_fusion.1
  161.8 2.9 convolution_convert_fusion.3
  164.7 146.8 %fusion.113 = (bf16[40,1728]{1,0:T(8,128)(2,1)S(1)}, bf16[48,576]{1,0:T(8,128)(2,1)S(1)}, bf16[40,1728]{1,0:T(8,128)(2,1)S(1)}, bf16[48,576]{1,0:T(8,128)(2,1)S(1)}) fusion(bf16[1152,1728]{1,0:T(8,128)(2,1)} %convolution_convert_fusion.1, bf16[1152,576]{1,0:T(8,128)(2,1)} %convolution_convert_fusion.3, bf16[1152,1728]{1,0:T(8,128)(2,1)} %convolution_convert_fusion, ...), kind=kCustom, calls=%all-reduce-scatter.4 | all-reduce-scatter fusion | flops 6193154 | bytes 11004416
  312.8 2.6 collective-permute-start.23
  315.5 2.4 collective-permute-start.11
  317.8 4.0 collective-permute-start.9
  323.2 4.0 collective-permute-start.7
  327.2 4.5 collective-permute-start.6
  331.7 2.3 collective-permute-start.5
  334.0 4.0 collective-permute-start.2
  338.0 1.9 collective-permute-start.4
  340.0 4.0 collective-permute-start.22
  345.3 2.2 collective-permute-start.20
  347.5 1.9 collective-permute-start.19
  349.4 3.4 collective-permute-start.18
  352.9 3.7 collective-permute-start.17
  356.6 1.9 collective-permute-start.16
  358.5 2.1 collective-permute-start.3
  361.8 2.0 concatenate.17
  363.8 3.7 collective-permute-start.1
  367.6 3.1 collective-permute-start
  370.7 3.5 collective-permute-start.14
  374.2 5.9 %concatenate.19 = bf16[420,576]{1,0:T(8,128)(2,1)S(1)} concatenate(bf16[36,576]{1,0:T(8,128)(2,1)S(1)} %collective-permute-done.23, bf16[48,576]{1,0:T(8,128)(2,1)S(1)} %collective-permute-done.22, bf16[48,576]{1,0:T(8,128)(2,1)} %copy-done.18, bf16[48,576]{1,0:T(8,128)(2,1)} %copy-done.19, bf16[48,576]{1,0:T(8,128)(2,1)} %copy-done.20, bf16[48,576]{1,0:T(8,128)(2,1)} %collective-permute-done.18, ...), dimensions={0} | concatenate | bytes 967680
  380.1 2.7 collective-permute-start.13
  382.8 3.3 collective-permute-start.12
  391.8 2.5 concatenate.18
  395.5 3.6 fusion.41
  400.1 2.3 fusion.75
  402.5 8.4 %reduce-scatter.27.cloned.1.call-done = bf16[144,36]{1,0:T(8,128)(2,1)} async-done(((bf16[576,36]{1,0:T(8,128)(2,1)}), bf16[144,36]{1,0:T(8,128)(2,1)}) %reduce-scatter.27.cloned.1.call-update) | async-done | bytes 10384
  412.4 27.0 %reduce-scatter.23.cloned.1.call-done = bf16[144,36]{1,0:T(8,128)(2,1)} async-done(((bf16[576,36]{1,0:T(8,128)(2,1)}), bf16[144,36]{1,0:T(8,128)(2,1)}) %reduce-scatter.23.cloned.1.call-update) | async-done | bytes 10384
  440.8 28.6 %reduce-scatter.25.cloned.1.call-done = bf16[432,36]{1,0:T(8,128)(2,1)} async-done(((bf16[1728,36]{1,0:T(8,128)(2,1)}), bf16[432,36]{1,0:T(8,128)(2,1)}) %reduce-scatter.25.cloned.1.call-update) | async-done | bytes 31120
  471.1 28.2 %reduce-scatter.21.cloned.1.call-done = bf16[432,36]{1,0:T(8,128)(2,1)} async-done(((bf16[1728,36]{1,0:T(8,128)(2,1)}), bf16[432,36]{1,0:T(8,128)(2,1)}) %reduce-scatter.21.cloned.1.call-update) | async-done | bytes 31120
  (127 shorter events, 41.0 us)
Async XLA Ops:
  7.2 25.9 %copy-start = (bf16[1152,576]{0,1:T(8,128)(2,1)S(1)}, bf16[1152,576]{0,1:T(8,128)(2,1)}, u32[]{:S(2)}) copy-start(bf16[1152,576]{0,1:T(8,128)(2,1)} %param.13) | copy-start | bytes 3981316
  14.8 11.8 %copy-start.2 = (bf16[1,1,256,1152]{3,2,1,0:T(8,128)(2,1)S(1)}, bf16[1,1,256,1152]{3,2,1,0:T(8,128)(2,1)}, u32[]{:S(2)}) copy-start(bf16[1,1,256,1152]{3,2,1,0:T(8,128)(2,1)} %param.8) | copy-start | bytes 1769476
  17.4 26.9 %all-to-all-start = ((bf16[32,2,4608]{2,1,0:T(2,128)(2,1)}), bf16[32,2,4608]{2,1,0:T(2,128)(2,1)}, u32[]{:S(2)}, u32[]{:S(2)}) async-start(bf16[32,2,4608]{2,1,0:T(2,128)(2,1)} %reshape.622), calls=%async_computation | async-start | bytes 1179648 | tf_op jit(solution)/shard_map/all_to_all | solution.py:92
  30.4 1.1 copy-start.16
  31.0 1.4 copy-start.11
  31.0 2.1 copy-start.3
  32.3 0.7 copy-start.14
  44.3 22.8 %all-to-all-start.1 = ((bf16[32,2,4608]{2,1,0:T(2,128)(2,1)}), bf16[32,2,4608]{2,1,0:T(2,128)(2,1)}, u32[]{:S(2)}, u32[]{:S(2)}) async-start(bf16[32,2,4608]{2,1,0:T(2,128)(2,1)} %reshape.620), calls=%async_computation.1 | async-start | bytes 1179648 | tf_op jit(solution)/shard_map/all_to_all | solution.py:100
  58.1 3.6 copy-start.13
  60.7 1.0 copy-start.4
  61.7 1.5 copy-start.22
  61.9 0.8 copy-start.10
  90.7 2.7 copy-start.6
  90.7 2.7 copy-start.7
  93.4 1.8 copy-start.8
  123.0 19.7 %all-to-all-start.2 = ((bf16[1,32,8,1152]{3,2,0,1:T(8,128)(2,1)}), bf16[1,32,8,1152]{3,2,0,1:T(8,128)(2,1)}, u32[]{:S(2)}, u32[]{:S(2)}) async-start(bf16[1,32,8,1152]{3,2,0,1:T(8,128)(2,1)} %fusion.58), calls=%async_computation.2 | async-start | bytes 1179648 | tf_op jit(solution)/shard_map/all_to_all | solution.py:105
  131.5 279.4 %reduce-scatter.27.cloned.1.call-start = ((), (), s32[]{:S(2)}) async-start(), calls=%async_computation.10 | async-start | bytes 184320
  131.8 3.0 copy-start.5
  131.8 3.0 copy-start.9
  142.7 1.8 copy-start.12
  144.5 1.2 copy-start.17
  158.4 3.4 copy-start.15
  164.7 195.9 %copy-start.21 = (u32[128]{0:T(128)S(1)}, u32[128]{0:T(128)}, u32[]{:S(2)}) copy-start(u32[128]{0:T(128)} %constant.26) | copy-start | bytes 1540
  311.5 20.2 %collective-permute-start.10 = (bf16[48,576]{1,0:T(8,128)(2,1)S(1)}, bf16[48,576]{1,0:T(8,128)(2,1)S(1)}, u32[]{:S(2)}, u32[]{:S(2)}) collective-permute-start(bf16[48,576]{1,0:T(8,128)(2,1)S(1)} %get-tuple-element.10), channel_id=1, source_target_pairs={{0,7},{1,8},{2,9},{3,10},{4,11},{5,12},{6,13},{7,14},{8,15},{9,16}... | collective-permute-start | bytes 165896
  312.8 10.3 %collective-permute-start.23 = (bf16[36,576]{1,0:T(8,128)(2,1)S(1)}, bf16[36,576]{1,0:T(8,128)(2,1)S(1)}, u32[]{:S(2)}, u32[]{:S(2)}) collective-permute-start(bf16[36,576]{1,0:T(8,128)(2,1)S(1)} %slice.33), channel_id=1, source_target_pairs={{0,8},{1,9},{2,10},{3,11},{4,12},{5,13},{6,14},{7,15},{8,16},{9,17... | collective-permute-start | bytes 124424
  315.5 11.7 %collective-permute-start.11 = (bf16[36,576]{1,0:T(8,128)(2,1)S(1)}, bf16[36,576]{1,0:T(8,128)(2,1)S(1)}, u32[]{:S(2)}, u32[]{:S(2)}) collective-permute-start(bf16[36,576]{1,0:T(8,128)(2,1)S(1)} %slice.31), channel_id=1, source_target_pairs={{0,8},{1,9},{2,10},{3,11},{4,12},{5,13},{6,14},{7,15},{8,16},{9,17... | collective-permute-start | bytes 124424
  317.8 16.2 %collective-permute-start.9 = (bf16[48,576]{1,0:T(8,128)(2,1)S(1)}, bf16[48,576]{1,0:T(8,128)(2,1)S(1)}, u32[]{:S(2)}, u32[]{:S(2)}) collective-permute-start(bf16[48,576]{1,0:T(8,128)(2,1)S(1)} %get-tuple-element.10), channel_id=1, source_target_pairs={{0,6},{1,7},{2,8},{3,9},{4,10},{5,11},{6,12},{7,13},{8,14},{9,15},... | collective-permute-start | bytes 165896
  321.8 16.2 %collective-permute-start.8 = (bf16[48,576]{1,0:T(8,128)(2,1)S(1)}, bf16[48,576]{1,0:T(8,128)(2,1)S(1)}, u32[]{:S(2)}, u32[]{:S(2)}) collective-permute-start(bf16[48,576]{1,0:T(8,128)(2,1)S(1)} %get-tuple-element.10), channel_id=1, source_target_pairs={{0,5},{1,6},{2,7},{3,8},{4,9},{5,10},{6,11},{7,12},{8,13},{9,14},{... | collective-permute-start | bytes 165896
  323.2 16.8 %collective-permute-start.7 = (bf16[48,576]{1,0:T(8,128)(2,1)S(1)}, bf16[48,576]{1,0:T(8,128)(2,1)S(1)}, u32[]{:S(2)}, u32[]{:S(2)}) collective-permute-start(bf16[48,576]{1,0:T(8,128)(2,1)S(1)} %get-tuple-element.10), channel_id=1, source_target_pairs={{0,4},{1,5},{2,6},{3,7},{4,8},{5,9},{6,10},{7,11},{8,12},{9,13},{1... | collective-permute-start | bytes 165896
  327.2 16.7 %collective-permute-start.6 = (bf16[48,576]{1,0:T(8,128)(2,1)S(1)}, bf16[48,576]{1,0:T(8,128)(2,1)S(1)}, u32[]{:S(2)}, u32[]{:S(2)}) collective-permute-start(bf16[48,576]{1,0:T(8,128)(2,1)S(1)} %get-tuple-element.10), channel_id=1, source_target_pairs={{0,3},{1,4},{2,5},{3,6},{4,7},{5,8},{6,9},{7,10},{8,11},{9,12},{10... | collective-permute-start | bytes 165896
  331.7 13.6 %collective-permute-start.5 = (bf16[48,576]{1,0:T(8,128)(2,1)S(1)}, bf16[48,576]{1,0:T(8,128)(2,1)S(1)}, u32[]{:S(2)}, u32[]{:S(2)}) collective-permute-start(bf16[48,576]{1,0:T(8,128)(2,1)S(1)} %get-tuple-element.10), channel_id=1, source_target_pairs={{0,2},{1,3},{2,4},{3,5},{4,6},{5,7},{6,8},{7,9},{8,10},{9,11},{10,... | collective-permute-start | bytes 165896
  334.0 48.8 %collective-permute-start.2 = (bf16[40,1728]{1,0:T(8,128)(2,1)S(1)}, bf16[40,1728]{1,0:T(8,128)(2,1)S(1)}, u32[]{:S(2)}, u32[]{:S(2)}) collective-permute-start(bf16[40,1728]{1,0:T(8,128)(2,1)S(1)} %get-tuple-element.9), channel_id=1, source_target_pairs={{0,3},{1,4},{2,5},{3,6},{4,7},{5,8},{6,9},{7,10},{8,11},{9,12},{10... | collective-permute-start | bytes 414728
  338.0 9.4 %collective-permute-start.4 = (bf16[48,576]{1,0:T(8,128)(2,1)S(1)}, bf16[48,576]{1,0:T(8,128)(2,1)S(1)}, u32[]{:S(2)}, u32[]{:S(2)}) collective-permute-start(bf16[48,576]{1,0:T(8,128)(2,1)S(1)} %get-tuple-element.10), channel_id=1, source_target_pairs={{0,1},{1,2},{2,3},{3,4},{4,5},{5,6},{6,7},{7,8},{8,9},{9,10},{10,1... | collective-permute-start | bytes 165896
  340.0 9.4 %collective-permute-start.22 = (bf16[48,576]{1,0:T(8,128)(2,1)S(1)}, bf16[48,576]{1,0:T(8,128)(2,1)S(1)}, u32[]{:S(2)}, u32[]{:S(2)}) collective-permute-start(bf16[48,576]{1,0:T(8,128)(2,1)S(1)} %get-tuple-element.12), channel_id=1, source_target_pairs={{0,7},{1,8},{2,9},{3,10},{4,11},{5,12},{6,13},{7,14},{8,15},{9,16}... | collective-permute-start | bytes 165896
  344.0 8.9 %collective-permute-start.21 = (bf16[48,576]{1,0:T(8,128)(2,1)S(1)}, bf16[48,576]{1,0:T(8,128)(2,1)S(1)}, u32[]{:S(2)}, u32[]{:S(2)}) collective-permute-start(bf16[48,576]{1,0:T(8,128)(2,1)S(1)} %get-tuple-element.12), channel_id=1, source_target_pairs={{0,6},{1,7},{2,8},{3,9},{4,10},{5,11},{6,12},{7,13},{8,14},{9,15},... | collective-permute-start | bytes 165896
  345.3 11.3 %collective-permute-start.20 = (bf16[48,576]{1,0:T(8,128)(2,1)S(1)}, bf16[48,576]{1,0:T(8,128)(2,1)S(1)}, u32[]{:S(2)}, u32[]{:S(2)}) collective-permute-start(bf16[48,576]{1,0:T(8,128)(2,1)S(1)} %get-tuple-element.12), channel_id=1, source_target_pairs={{0,5},{1,6},{2,7},{3,8},{4,9},{5,10},{6,11},{7,12},{8,13},{9,14},{... | collective-permute-start | bytes 165896
  347.5 11.0 %collective-permute-start.19 = (bf16[48,576]{1,0:T(8,128)(2,1)S(1)}, bf16[48,576]{1,0:T(8,128)(2,1)S(1)}, u32[]{:S(2)}, u32[]{:S(2)}) collective-permute-start(bf16[48,576]{1,0:T(8,128)(2,1)S(1)} %get-tuple-element.12), channel_id=1, source_target_pairs={{0,4},{1,5},{2,6},{3,7},{4,8},{5,9},{6,10},{7,11},{8,12},{9,13},{1... | collective-permute-start | bytes 165896
  349.4 14.4 %collective-permute-start.18 = (bf16[48,576]{1,0:T(8,128)(2,1)S(1)}, bf16[48,576]{1,0:T(8,128)(2,1)}, u32[]{:S(2)}, u32[]{:S(2)}) collective-permute-start(bf16[48,576]{1,0:T(8,128)(2,1)S(1)} %get-tuple-element.12), channel_id=1, source_target_pairs={{0,3},{1,4},{2,5},{3,6},{4,7},{5,8},{6,9},{7,10},{8,11},{9,12},{10... | collective-permute-start | bytes 165896
  352.9 17.8 %copy-start.18 = (bf16[48,576]{1,0:T(8,128)(2,1)}, bf16[48,576]{1,0:T(8,128)(2,1)S(1)}, u32[]{:S(2)}) copy-start(bf16[48,576]{1,0:T(8,128)(2,1)S(1)} %collective-permute-done.21) | copy-start | bytes 165892
  352.9 14.7 %collective-permute-start.17 = (bf16[48,576]{1,0:T(8,128)(2,1)S(1)}, bf16[48,576]{1,0:T(8,128)(2,1)}, u32[]{:S(2)}, u32[]{:S(2)}) collective-permute-start(bf16[48,576]{1,0:T(8,128)(2,1)S(1)} %get-tuple-element.12), channel_id=1, source_target_pairs={{0,2},{1,3},{2,4},{3,5},{4,6},{5,7},{6,8},{7,9},{8,10},{9,11},{10,... | collective-permute-start | bytes 165896
  356.6 14.1 %copy-start.19 = (bf16[48,576]{1,0:T(8,128)(2,1)}, bf16[48,576]{1,0:T(8,128)(2,1)S(1)}, u32[]{:S(2)}) copy-start(bf16[48,576]{1,0:T(8,128)(2,1)S(1)} %collective-permute-done.20) | copy-start | bytes 165892
  356.6 14.1 %collective-permute-start.16 = (bf16[48,576]{1,0:T(8,128)(2,1)S(1)}, bf16[48,576]{1,0:T(8,128)(2,1)}, u32[]{:S(2)}, u32[]{:S(2)}) collective-permute-start(bf16[48,576]{1,0:T(8,128)(2,1)S(1)} %get-tuple-element.12), channel_id=1, source_target_pairs={{0,1},{1,2},{2,3},{3,4},{4,5},{5,6},{6,7},{7,8},{8,9},{9,10},{10,1... | collective-permute-start | bytes 165896
  358.5 12.2 %copy-start.20 = (bf16[48,576]{1,0:T(8,128)(2,1)}, bf16[48,576]{1,0:T(8,128)(2,1)S(1)}, u32[]{:S(2)}) copy-start(bf16[48,576]{1,0:T(8,128)(2,1)S(1)} %collective-permute-done.19) | copy-start | bytes 165892
  358.5 21.6 %collective-permute-start.3 = (bf16[4,1728]{1,0:T(4,128)(2,1)S(1)}, bf16[4,1728]{1,0:T(4,128)(2,1)S(1)}, u32[]{:S(2)}, u32[]{:S(2)}) collective-permute-start(bf16[4,1728]{1,0:T(4,128)(2,1)S(1)} %slice.30), channel_id=1, source_target_pairs={{0,4},{1,5},{2,6},{3,7},{4,8},{5,9},{6,10},{7,11},{8,12},{9,13},{1... | collective-permute-start | bytes 41480
  363.8 23.2 %collective-permute-start.1 = (bf16[40,1728]{1,0:T(8,128)(2,1)S(1)}, bf16[40,1728]{1,0:T(8,128)(2,1)S(1)}, u32[]{:S(2)}, u32[]{:S(2)}) collective-permute-start(bf16[40,1728]{1,0:T(8,128)(2,1)S(1)} %get-tuple-element.9), channel_id=1, source_target_pairs={{0,2},{1,3},{2,4},{3,5},{4,6},{5,7},{6,8},{7,9},{8,10},{9,11},{10,... | collective-permute-start | bytes 414728
  367.6 22.5 %collective-permute-start = (bf16[40,1728]{1,0:T(8,128)(2,1)S(1)}, bf16[40,1728]{1,0:T(8,128)(2,1)}, u32[]{:S(2)}, u32[]{:S(2)}) collective-permute-start(bf16[40,1728]{1,0:T(8,128)(2,1)S(1)} %get-tuple-element.9), channel_id=1, source_target_pairs={{0,1},{1,2},{2,3},{3,4},{4,5},{5,6},{6,7},{7,8},{8,9},{9,10},{10,1... | collective-permute-start | bytes 414728
  370.7 21.1 %collective-permute-start.14 = (bf16[40,1728]{1,0:T(8,128)(2,1)S(1)}, bf16[40,1728]{1,0:T(8,128)(2,1)S(1)}, u32[]{:S(2)}, u32[]{:S(2)}) collective-permute-start(bf16[40,1728]{1,0:T(8,128)(2,1)S(1)} %get-tuple-element.11), channel_id=1, source_target_pairs={{0,3},{1,4},{2,5},{3,6},{4,7},{5,8},{6,9},{7,10},{8,11},{9,12},{10... | collective-permute-start | bytes 414728
  380.1 11.7 %collective-permute-start.13 = (bf16[40,1728]{1,0:T(8,128)(2,1)S(1)}, bf16[40,1728]{1,0:T(8,128)(2,1)}, u32[]{:S(2)}, u32[]{:S(2)}) collective-permute-start(bf16[40,1728]{1,0:T(8,128)(2,1)S(1)} %get-tuple-element.11), channel_id=1, source_target_pairs={{0,2},{1,3},{2,4},{3,5},{4,6},{5,7},{6,8},{7,9},{8,10},{9,11},{10,... | collective-permute-start | bytes 414728
  382.8 9.0 %collective-permute-start.12 = (bf16[40,1728]{1,0:T(8,128)(2,1)S(1)}, bf16[40,1728]{1,0:T(8,128)(2,1)}, u32[]{:S(2)}, u32[]{:S(2)}) collective-permute-start(bf16[40,1728]{1,0:T(8,128)(2,1)S(1)} %get-tuple-element.11), channel_id=1, source_target_pairs={{0,1},{1,2},{2,3},{3,4},{4,5},{5,6},{6,7},{7,8},{8,9},{9,10},{10,1... | collective-permute-start | bytes 414728
  386.9 52.4 %reduce-scatter.23.cloned.1.call-start = ((), (), s32[]{:S(2)}) async-start(), calls=%async_computation.8 | async-start | bytes 184320
  387.0 4.8 collective-permute-start.15
  389.8 79.6 %reduce-scatter.25.cloned.1.call-start = ((), (), s32[]{:S(2)}) async-start(), calls=%async_computation.9 | async-start | bytes 552960
  395.5 103.8 %reduce-scatter.21.cloned.1.call-start = ((), (), s32[]{:S(2)}) async-start(), calls=%async_computation.7 | async-start | bytes 552960
  400.1 100.8 %copy-start.1 = (bf16[1152,576]{0,1:T(8,128)(2,1)S(1)}, bf16[1152,576]{0,1:T(8,128)(2,1)}, u32[]{:S(2)}) copy-start(bf16[1152,576]{0,1:T(8,128)(2,1)} %param.13) | copy-start | bytes 3981316
Sparse Core Ops, SparseCore 0:
  387.1 23.7 reduce-scatter.26
  413.4 25.8 reduce-scatter.22
  442.0 27.3 reduce-scatter.24
  471.9 27.3 reduce-scatter.20
where the time goes:
time: 516 us; the launch traced here: 508 us
  blocking collectives  147 us (28%)
  waiting for transfers between devices  96.9 us (19%)
  starting transfers between devices  93.8 us (18%)
  local copies, waits for them, and re-layouts  64.2 us (12%)
  matrix products  63.2 us (12%)
  other arithmetic  26.8 us (5%)
  between operations  16 us (3%)
    unnamed x1, blocking collectives  147 us
    unnamed x32, waiting for transfers between devices  92.3 us
    unnamed x28, starting transfers between devices  67 us
    unnamed x71, local copies, waits for them, and re-layouts  41.8 us
    unnamed x2, other arithmetic  11 us
  transfers between devices with their start and end apart: 31, of which 5 were waited for; matrix products, arithmetic and copies ran while one was open for 12% of the time, Pallas kernels for 0%

commit v1 on v0

v1 whole, which is shorter than its diff:
```python
import jax
import jax.numpy as jnp
from jax import lax
from jax.experimental import pallas as pl
from jax.experimental.pallas import tpu as pltpu
from jax.sharding import PartitionSpec as P

D = 1152
H = 8
HD = 72
INNER = 576
T = 256
NS = 32
RB = 40
MESH = pl.DeviceIdType.MESH
BF = jnp.bfloat16
F32 = jnp.float32
SCALE = HD ** (-0.5)
KEEP = 1.0 / 0.9


def nt(a, b):
    return lax.dot_general(a, b, (((1,), (1,)), ((), ())), preferred_element_type=F32)


def tn(a, b):
    return lax.dot_general(a, b, (((0,), (0,)), ((), ())), preferred_element_type=F32)


def nn(a, b):
    return jnp.dot(a, b, preferred_element_type=F32)


SCRATCH = dict(
    x=((32, 8, D), BF),
    ks=((32, 8, D), jnp.int32),
    kt=((32, 8, D), jnp.int32),
    wqs=((D, 3 * INNER), BF),
    wos=((D, INNER), BF),
    wqt=((D, 3 * INNER), BF),
    wot=((D, INNER), BF),
    go=((NS, 8, D), BF),
    y_out=((NS, 8, D), BF),
    y_in=((NS, 8, D), BF),
    d_out=((NS, 8, D), BF),
    d_in=((NS, 8, D), BF),
    normed_s=((T, D), BF),
    normed_t=((T, D), BF),
    qkv=((T, 3 * INNER), BF),
    hs_s=((24, T, 128), BF),
    hs_t=((24, T, 128), BF),
    probs=((H, T, T), F32),
    mh_s=((H, T, 128), BF),
    mh_t=((H, T, 128), BF),
    mixed=((T, INNER), BF),
    dproj=((T, D), BF),
    dmix=((T, INNER), BF),
    dmh=((H, T, 128), BF),
    dh=((24, T, 128), BF),
    dqkv=((T, 3 * INNER), BF),
    dn=((T, D), F32),
    dsel=((2, 2, T, D), BF),
    dsel_in=((2, T, D), BF),
    perm=((32 * RB, D), BF),
    lt=((2, 32 * RB, T), BF),
    lt_in=((2, 2, 32 * RB, T), BF),
    grad=((2, 8, 4, RB, D), BF),
    r1=((2, 2, 2, 2, RB, D), BF),
    r2=((2, 2, 2, 4, RB, D), BF),
    hsum=((2, 2, 4, RB, D), BF),
    r3=((2, 2, 3, RB, D), BF),
    zsum=((2, 2, 2, RB, INNER), BF),
    r4=((2, 3, RB, INNER), BF),
    dx=((32, 8, D), BF),
)
SEMS = dict(
    load=(8,),
    store=(1,),
    a2a_s=(3, 31),
    a2a_r=(3, 31),
    core_s=(2, 3),
    core_r=(2, 3),
    r1_s=(2, 2, 2),
    r1_r=(2, 2, 2),
    r2_s=(2, 2, 2, 2),
    r2_r=(2, 2, 2, 2),
    r3_s=(2, 2, 3),
    r3_r=(2, 2, 3),
    r4_s=(2, 3),
    r4_r=(2, 3),
)


class Refs:
    pass


def body(*refs):
    ins, outs, rest = refs[:8], refs[8:13], refs[13:]
    m = Refs()
    for name, ref in zip(SCRATCH, rest[: len(SCRATCH)]):
        setattr(m, name, ref)
    for name, ref in zip(SEMS, rest[len(SCRATCH):]):
        setattr(m, name + "_sem", ref)
    dx_hbm, gqs, gos, gqt, got = outs

    dp = lax.axis_index("dp")
    me = lax.axis_index("seq")
    zh, core = dp // 2, lax.rem(dp, 2)
    cx, zl, cy = me // 8, lax.rem(me // 4, 2), lax.rem(me, 4)
    cz = zh * 2 + zl

    def place(x, y, z):
        return ((z // 2) * 2 + core, x * 8 + lax.rem(z, 2) * 4 + y)

    dests = (m.x, None, m.ks, m.kt, m.wqs, m.wos, m.wqt, m.wot)
    loads = [
        None if dst is None else pltpu.make_async_copy(src, dst, m.load_sem.at[i])
        for i, (src, dst) in enumerate(zip(ins, dests))
    ]
    for i in (0, 4, 2, 5, 7, 3, 6):
        loads[i].start()

    barrier = pltpu.get_barrier_semaphore()

    def greet(d, carry):
        pl.semaphore_signal(
            barrier, inc=1, device_id=(dp, lax.rem(me + d, NS)), device_id_type=MESH
        )
        return carry

    lax.fori_loop(1, NS, greet, 0)
    other_core = (zh * 2 + 1 - core, me)
    pl.semaphore_signal(barrier, inc=1, device_id=other_core, device_id_type=MESH)
    far = (1 - zh) * 2 + core
    pl.semaphore_signal(barrier, inc=1, device_id=(far, me), device_id_type=MESH)
    pl.semaphore_signal(
        barrier, inc=1, device_id=(far, cx * 8 + (1 - zl) * 4 + cy), device_id_type=MESH
    )

    def a2a_copy(k, src, dst, d):
        to = lax.rem(me + d, NS)
        return pltpu.make_async_remote_copy(
            src_ref=src.at[to],
            dst_ref=dst.at[me],
            send_sem=m.a2a_s_sem.at[k, d - 1],
            recv_sem=m.a2a_r_sem.at[k, d - 1],
            device_id=(dp, to),
            device_id_type=MESH,
        )

    def a2a_start(k, src, dst):
        def step(d, carry):
            a2a_copy(k, src, dst, d).start()
            return carry

        lax.fori_loop(1, NS, step, 0)

    def a2a_wait(k, src, dst):
        def step(d, carry):
            frm = lax.rem(me + NS - d, NS)
            pltpu.make_async_remote_copy(
                src_ref=src.at[frm],
                dst_ref=dst.at[frm],
                send_sem=m.a2a_s_sem.at[k, d - 1],
                recv_sem=m.a2a_r_sem.at[k, d - 1],
                device_id=(dp, frm),
                device_id_type=MESH,
            ).wait_recv()
            return carry

        lax.fori_loop(1, NS, step, 0)

    def a2a_drain(k, src, dst):
        def step(d, carry):
            a2a_copy(k, src, dst, d).wait_send()
            return carry

        lax.fori_loop(1, NS, step, 0)

    def rows(fn):
        def step(r, carry):
            fn(pl.ds(pl.multiple_of(r * 32, 32), 32), pl.ds(r * 4, 4))
            return carry

        lax.fori_loop(0, 8, step, 0)

    def flat(ref, blk):
        return ref[blk].astype(F32).reshape(32, D)

    def inv_of(zf):
        return lax.rsqrt(jnp.mean(zf * zf, axis=-1, keepdims=True) + 1e-06)

    def normalize(src, dst):
        def fn(r, blk):
            zf = flat(src, blk)
            dst[r, :] = (zf * inv_of(zf)).astype(BF)

        rows(fn)

    def split_heads(src, dst, n):
        for j in range(n):
            v = src[:, HD * j: HD * (j + 1)]
            dst[j] = jnp.concatenate([v, jnp.zeros((T, 128 - HD), BF)], axis=1)

    def qkv_heads(normed, w, hs):
        for lo, hi in ((0, 512), (512, 1024), (1024, 1536), (1536, 1728)):
            m.qkv[:, lo:hi] = nn(normed[...], w[:, lo:hi]).astype(BF)
        split_heads(m.qkv, hs, 24)

    def d_proj_mix(dy, keep, wo):
        def fn(r, blk):
            m.dproj[r, :] = (flat(dy, blk) * (flat(keep, blk) * KEEP)).astype(BF)

        rows(fn)
        m.dmix[...] = nn(m.dproj[...], wo[...]).astype(BF)
        split_heads(m.dmix, m.dmh, H)

    def softmax(q, k, mask):
        e = jnp.exp(nt(q, k) * SCALE)
        if mask is not None:
            e = jnp.where(mask, e, 0.0)
        return e / jnp.sum(e, axis=-1, keepdims=True)

    def attention_backward(h, p, p_low, q, k, v):
        dm = m.dmh[h]
        dp_ = nt(dm, v)
        ds = (p * (dp_ - jnp.sum(p * dp_, axis=-1, keepdims=True)) * SCALE).astype(BF)
        m.dh[h] = nn(ds, k).astype(BF)
        m.dh[h + 8] = tn(ds, q).astype(BF)
        m.dh[h + 16] = tn(p_low, dm).astype(BF)

    def gather_columns(sec, mh):
        for j in range(24):
            m.dqkv[:, HD * j: HD * (j + 1)] = m.dh[j][:, :HD]
        for c in range(2):
            for i in range(6):
                m.dsel[sec, c, :, HD * i: HD * (i + 1)] = m.dh[6 * c + i][:, :HD]
                lo = 432 + HD * i
                m.dsel[sec, c, :, lo: lo + HD] = m.dh[12 + 6 * c + i][:, :HD]
            for i, h in enumerate((2 * c, 2 * c + 1, 4 + 2 * c, 5 + 2 * c)):
                lo = 864 + HD * i
                m.dsel[sec, c, :, lo: lo + HD] = mh[h][:, :HD]

    def input_backward(src, dy, dst, wq):
        for n in range(3):
            m.dn[:, 384 * n: 384 * (n + 1)] = nt(m.dqkv[...], wq[384 * n: 384 * (n + 1), :])

        def fn(r, blk):
            zf = flat(src, blk)
            inv = inv_of(zf)
            c = zf * inv
            dn = m.dn[r, :]
            dz = flat(dy, blk) + inv * (dn - c * jnp.mean(dn * c, axis=-1, keepdims=True))
            dst[blk] = dz.reshape(4, 8, D).astype(BF)

        rows(fn)

    def core_copies(sec):
        pairs = (
            (m.lt.at[0], m.lt_in.at[sec, 0]),
            (m.lt.at[1], m.lt_in.at[sec, 1]),
            (m.dsel.at[sec, 1 - core], m.dsel_in.at[sec]),
        )
        return [
            pltpu.make_async_remote_copy(
                src_ref=src,
                dst_ref=dst,
                send_sem=m.core_s_sem.at[sec, i],
                recv_sem=m.core_r_sem.at[sec, i],
                device_id=other_core,
                device_id_type=MESH,
            )
            for i, (src, dst) in enumerate(pairs)
        ]

    def transpose_rows(i, src):
        def step(n, carry):
            r = pl.ds(pl.multiple_of(n * 320, 320), 320)
            m.lt[i, r, :] = nt(m.perm[r, :], src[...]).astype(BF)
            return carry

        lax.fori_loop(0, 4, step, 0)

    def weight_grads(sec):
        def step(n, carry):
            r = pl.ds(pl.multiple_of(n * 320, 320), 320)
            for i, lo, hi in ((0, 0, 384), (0, 384, 864), (1, 864, 1152)):
                acc = nn(m.lt[i, r, :], m.dsel[sec, core, :, lo:hi])
                acc = acc + nn(m.lt_in[sec, i, r, :], m.dsel_in[sec, :, lo:hi])
                m.grad[sec, pl.ds(n * 2, 2), :, :, lo:hi] = acc.reshape(
                    2, 4, RB, hi - lo
                ).astype(BF)
            return carry

        lax.fori_loop(0, 4, step, 0)

    def ring(o):
        return cx if o == 0 else cy

    def on_first(o, i):
        return place(i, cy, cz) if o == 0 else place(cx, i, cz)

    def on_second(o, i):
        return place(cx, i, cz) if o == 0 else place(i, cy, cz)

    def remote(src, dst, ssem, rsem, to):
        return pltpu.make_async_remote_copy(
            src_ref=src, dst_ref=dst, send_sem=ssem, recv_sem=rsem, device_id=to, device_id_type=MESH
        )

    def first_copies(sec, o):
        i = ring(o)
        up, dn, opp = lax.rem(i + 1, 4), lax.rem(i + 3, 4), lax.rem(i + 2, 4)
        g = m.grad
        one = [
            remote(g.at[sec, o * 4 + opp, 0:2], m.r1.at[sec, o, 0],
                   m.r1_s_sem.at[sec, o, 0], m.r1_r_sem.at[sec, o, 0], on_first(o, up)),
            remote(g.at[sec, o * 4 + opp, 2:4], m.r1.at[sec, o, 1],
                   m.r1_s_sem.at[sec, o, 1], m.r1_r_sem.at[sec, o, 1], on_first(o, dn)),
        ]
        two = [
            [
                remote(g.at[sec, o * 4 + up, 2 * b: 2 * b + 2], m.r2.at[sec, o, 0, 2 * b: 2 * b + 2],
                       m.r2_s_sem.at[sec, o, 0, b], m.r2_r_sem.at[sec, o, 0, b], on_first(o, up))
                for b in range(2)
            ],
            [
                remote(g.at[sec, o * 4 + dn, 2 * b: 2 * b + 2], m.r2.at[sec, o, 1, 2 * b: 2 * b + 2],
                       m.r2_s_sem.at[sec, o, 1, b], m.r2_r_sem.at[sec, o, 1, b], on_first(o, dn))
                for b in range(2)
            ],
        ]
        return one, two, up, dn, i

    def reduce_start(sec):
        for o in range(2):
            one, two, up, dn, i = first_copies(sec, o)
            one[0].start()
            one[1].start()
            two[0][1].start()
            two[1][0].start()

    def reduce_relay(sec):
        for o in range(2):
            one, two, up, dn, i = first_copies(sec, o)
            for side, chunk, b in ((0, up, 0), (1, dn, 1)):
                one[side].wait_recv()
                for e in range(2 * b, 2 * b + 2):
                    acc = m.grad[sec, o * 4 + chunk, e].astype(F32)
                    acc = acc + m.r1[sec, o, side, e - 2 * b].astype(F32)
                    m.grad[sec, o * 4 + chunk, e] = acc.astype(BF)
                two[side][b].start()

    def second_copies(sec, o):
        j = ring(1 - o)
        return [
            remote(m.hsum.at[sec, o, lax.rem(j + d, 4)], m.r3.at[sec, o, d - 1],
                   m.r3_s_sem.at[sec, o, d - 1], m.r3_r_sem.at[sec, o, d - 1],
                   on_second(o, lax.rem(j + d, 4)))
            for d in (1, 2, 3)
        ]

    def reduce_second(sec):
        for o in range(2):
            one, two, up, dn, i = first_copies(sec, o)
            for side in two:
                for c in side:
                    c.wait_recv()
            for e in range(4):
                acc = m.grad[sec, o * 4 + i, e].astype(F32)
                acc = acc + m.r2[sec, o, 0, e].astype(F32)
                acc = acc + m.r2[sec, o, 1, e].astype(F32)
                m.hsum[sec, o, e] = acc.astype(BF)
            for c in second_copies(sec, o):
                c.start()

    def z_copies(sec):
        copies = []
        for d in (1, 2, 3):
            z = lax.rem(cz + d, 4)
            copies.append(
                remote(m.zsum.at[sec, lax.rem(z, 2), z // 2], m.r4.at[sec, d - 1],
                       m.r4_s_sem.at[sec, d - 1], m.r4_r_sem.at[sec, d - 1], place(cx, cy, z))
            )
        return copies

    def reduce_z(sec):
        for o in range(2):
            for c in second_copies(sec, o):
                c.wait_recv()
            acc = m.hsum[sec, o, ring(1 - o)].astype(F32)
            for d in range(3):
                acc = acc + m.r3[sec, o, d].astype(F32)
            for z in range(2):
                m.zsum[sec, o, z] = jnp.concatenate(
                    [acc[:, 432 * z: 432 * (z + 1)], acc[:, 864 + 144 * z: 864 + 144 * (z + 1)]],
                    axis=1,
                ).astype(BF)
        for c in z_copies(sec):
            c.start()

    def reduce_end(sec, gq, gout):
        for c in z_copies(sec):
            c.wait_recv()
        acc = m.zsum[sec, zl, zh].astype(F32)
        for d in range(3):
            acc = acc + m.r4[sec, d].astype(F32)
        gq[...] = acc[0:36, 0:432]
        gout[...] = acc[0:36, 432:576]

    def reduce_drain(sec):
        for c in core_copies(sec)[2:]:
            c.wait_send()
        for o in range(2):
            one, two, up, dn, i = first_copies(sec, o)
            for c in one + two[0] + two[1]:
                c.wait_send()
            for c in second_copies(sec, o):
                c.wait_send()
        for c in z_copies(sec):
            c.wait_send()

    loads[0].wait()
    normalize(m.x, m.normed_s)
    pl.semaphore_wait(barrier, NS + 2)
    a2a_start(0, ins[1], m.go)
    own = pltpu.make_async_copy(ins[1].at[me], m.go.at[me], m.load_sem.at[1])
    own.start()
    loads[4].wait()
    qkv_heads(m.normed_s, m.wqs, m.hs_s)

    def spatial_head(h, carry):
        p = softmax(m.hs_s[h], m.hs_s[h + 8], None)
        m.probs[h] = p
        m.mh_s[h] = nn(p.astype(BF), m.hs_s[h + 16]).astype(BF)
        return carry

    lax.fori_loop(0, H, spatial_head, 0)
    for h in range(H):
        m.mixed[:, HD * h: HD * (h + 1)] = m.mh_s[h][:, :HD]
    loads[2].wait()
    loads[5].wait()
    for n in range(3):
        c = slice(384 * n, 384 * (n + 1))
        proj = nt(m.mixed[...], m.wos[c, :]).reshape(32, 8, 384)
        keep = m.ks[:, :, c].astype(F32) * KEEP
        m.y_out[:, :, c] = (m.x[:, :, c].astype(F32) + proj * keep).astype(BF)
    a2a_start(1, m.y_out, m.y_in)
    m.y_in[me] = m.y_out[me]

    def perm_step(n, carry):
        blocks = []
        for k in (2 * n, 2 * n + 1):
            o, a, b = k // 16, lax.rem(k // 4, 4), lax.rem(k, 4)
            x = a * (1 - o) + b * o
            y = b * (1 - o) + a * o
            s = x * 8 + o * 4 + y
            row = lax.broadcasted_iota(jnp.int32, (RB, D), 0)
            col = lax.broadcasted_iota(jnp.int32, (RB, D), 1)
            hit = (col == row + 36 * s) & (row < 36)
            blocks.append(jnp.where(hit, 1.0, 0.0))
        both = jnp.concatenate(blocks, axis=0).astype(BF)
        m.perm[pl.ds(pl.multiple_of(n * 80, 80), 80), :] = both
        return carry

    lax.fori_loop(0, NS // 2, perm_step, 0)

    own.wait()
    a2a_wait(0, m.go, m.go)
    loads[3].wait()
    loads[7].wait()
    d_proj_mix(m.go, m.kt, m.wot)
    transpose_rows(1, m.dproj)
    core_copies(0)[1].start()
    a2a_wait(1, m.y_out, m.y_in)
    normalize(m.y_in, m.normed_t)
    loads[6].wait()
    qkv_heads(m.normed_t, m.wqt, m.hs_t)

    def temporal_head(h, carry):
        i = lax.broadcasted_iota(jnp.int32, (T, T), 0)
        j = lax.broadcasted_iota(jnp.int32, (T, T), 1)
        mask = ((i - j) & 7) == 0
        q, k, v = m.hs_t[h], m.hs_t[h + 8], m.hs_t[h + 16]
        p = softmax(q, k, mask)
        p_low = p.astype(BF)
        m.mh_t[h] = nn(p_low, v).astype(BF)
        attention_backward(h, p, p_low, q, k, v)
        return carry

    lax.fori_loop(0, H, temporal_head, 0)
    gather_columns(0, m.mh_t)
    core_copies(0)[2].start()
    input_backward(m.y_in, m.go, m.d_out, m.wqt)
    a2a_start(2, m.d_out, m.d_in)
    m.d_in[me] = m.d_out[me]
    transpose_rows(0, m.normed_t)
    core_copies(0)[0].start()
    for c in core_copies(0):
        c.wait_recv()
    weight_grads(0)
    for c in core_copies(0)[:2]:
        c.wait_send()

    transpose_rows(0, m.normed_s)
    core_copies(1)[0].start()
    a2a_wait(2, m.d_out, m.d_in)
    reduce_start(0)
    d_proj_mix(m.d_in, m.ks, m.wos)
    transpose_rows(1, m.dproj)
    core_copies(1)[1].start()
    reduce_relay(0)

    def spatial_back(h, carry):
        p = m.probs[h]
        attention_backward(h, p, p.astype(BF), m.hs_s[h], m.hs_s[h + 8], m.hs_s[h + 16])
        return carry

    lax.fori_loop(0, H, spatial_back, 0)
    gather_columns(1, m.mh_s)
    core_copies(1)[2].start()
    reduce_second(0)
    for c in core_copies(1):
        c.wait_recv()
    weight_grads(1)
    reduce_start(1)
    reduce_z(0)
    input_backward(m.x, m.d_in, m.dx, m.wqs)
    store = pltpu.make_async_copy(m.dx, dx_hbm, m.store_sem.at[0])
    store.start()
    reduce_end(0, gqt, got)
    reduce_relay(1)
    reduce_second(1)
    reduce_z(1)
    reduce_end(1, gqs, gos)

    a2a_drain(0, ins[1], m.go)
    a2a_drain(1, m.y_out, m.y_in)
    a2a_drain(2, m.d_out, m.d_in)
    for c in core_copies(1)[:2]:
        c.wait_send()
    reduce_drain(0)
    reduce_drain(1)
    store.wait()


def shards(
    block_input,
    out_grad,
    spatial_keep,
    temporal_keep,
    spatial_qkv,
    spatial_out,
    temporal_qkv,
    temporal_out,
):
    hbm = pl.BlockSpec(memory_space=pl.ANY)
    vmem = pl.BlockSpec(memory_space=pltpu.VMEM)
    outs = pl.pallas_call(
        body,
        out_shape=(
            jax.ShapeDtypeStruct((32, 8, D), BF),
            jax.ShapeDtypeStruct((36, 432), F32),
            jax.ShapeDtypeStruct((36, 144), F32),
            jax.ShapeDtypeStruct((36, 432), F32),
            jax.ShapeDtypeStruct((36, 144), F32),
        ),
        in_specs=[hbm] * 8,
        out_specs=(hbm, vmem, vmem, vmem, vmem),
        scratch_shapes=[pltpu.VMEM(s, d) for s, d in SCRATCH.values()]
        + [pltpu.SemaphoreType.DMA(s) for s in SEMS.values()],
        compiler_params=pltpu.CompilerParams(
            collective_id=0, has_side_effects=True, vmem_limit_bytes=63 * 2**20
        ),
    )(
        block_input.reshape(32, 8, D),
        out_grad.reshape(32, 8, D),
        spatial_keep.reshape(32, 8, D),
        temporal_keep.reshape(32, 8, D),
        spatial_qkv,
        spatial_out,
        temporal_qkv,
        temporal_out,
    )
    return (outs[0].reshape(1, 1, T, D),) + tuple(outs[1:])


def solution(mesh):
    return jax.shard_map(
        shards,
        mesh=mesh,
        in_specs=(
            P("dp", "seq", None, None),
            P("dp", "seq", None, None),
            P("dp", "seq", None, None),
            P("dp", None, "seq", None),
            P(),
            P(),
            P(),
            P(),
        ),
        out_specs=(
            P("dp", "seq", None, None),
            P("seq", "dp"),
            P("seq", "dp"),
            P("seq", "dp"),
            P("seq", "dp"),
        ),
        check_vma=False,
    )
```

time: 516 us -> 122 us (0.24); the launches traced: 508 us -> 121 us
  blocking collectives: 147 us -> 0 us
  Pallas kernels: 0 us -> 97.2 us
  waiting for transfers between devices: 96.9 us -> 0 us
  starting transfers between devices: 93.8 us -> 0 us
  matrix products: 63.2 us -> 0 us
  local copies, waits for them, and re-layouts: 64.2 us -> 23.4 us
  other arithmetic: 26.8 us -> 0 us
  between operations: 16 us -> 0.67 us
    unnamed x1 -> x0, blocking collectives: 147 us -> none
    pallas_call x0 -> x1, Pallas kernels: none -> 97.2 us  [shards(): pl.pallas_call(body, out_shape=(jax.ShapeDtypeStruct((32, 8, D), BF), jax...]
    unnamed x32 -> x0, waiting for transfers between devices: 92.3 us -> none
    unnamed x28 -> x0, starting transfers between devices: 67 us -> none
    dot_general x22 -> x0, matrix products: 60.1 us -> none  [the longest x2 9.2 us: section_backward(): jnp.einsum('aehij,aiehc->ajehc', d_scores, query, preferred_element_type=...]
    all_to_all x3 -> x0, starting transfers between devices: 26.8 us -> none  [the longest x1 9.2 us: shards(): lax.all_to_all(out_grad, 'seq', split_axis=2, concat_axis=1, tiled=True)]
    unnamed x71 -> x15, local copies, waits for them, and re-layouts: 41.8 us -> 23.4 us
    convert_element_type x9 -> x0, other arithmetic: 13.2 us -> none  [the longest x1 2.94 us: shards(): d_first.astype(jnp.bfloat16)]
  transfers between devices with their start and end apart: 31 -> 0, of which waited for: 5 -> 0; matrix products, arithmetic and copies ran while one was open for 12% -> 0% of each run, Pallas kernels for 0% -> 0%
where the time goes in v1:
time: 122 us; the launch traced here: 121 us
  Pallas kernels  97.2 us (80%)
  local copies, waits for them, and re-layouts  23.4 us (19%)
    pallas_call x1, Pallas kernels, shards(): pl.pallas_call(body, out_shape=(jax.ShapeDtypeStruct((32, 8, D), BF), jax...  97.2 us
    unnamed x15, local copies, waits for them, and re-layouts  23.4 us

profile of v1, /device:TPU:0, one launch (start us, length us, event | category | flops | bytes accessed | tf_op | source)
XLA Modules:
  0.0 121.3 jit_solution(8119856032217076343)
XLA Ops:
  0.6 0.0 copy-start
  0.6 2.8 %copy.14.refs_5_ = bf16[1152,576]{1,0:T(8,128)(2,1)} copy(bf16[1152,576]{0,1:T(8,128)(2,1)} %param.13) | data formatting | bytes 2654208 | tf_op args[5]
  3.4 0.0 copy-done
  3.4 1.6 %copy.16.refs_7_ = bf16[1152,576]{1,0:T(8,128)(2,1)} copy(bf16[1152,576]{0,1:T(8,128)(2,1)S(1)} %copy-done) | data formatting | bytes 2654208 | tf_op args[7]
  5.0 6.5 %copy.13.refs_4_ = bf16[1152,1728]{1,0:T(8,128)(2,1)} copy(bf16[1152,1728]{0,1:T(8,128)(2,1)} %param.12) | data formatting | bytes 7962624 | tf_op args[4]
  11.5 6.4 %copy.15.refs_6_ = bf16[1152,1728]{1,0:T(8,128)(2,1)} copy(bf16[1152,1728]{0,1:T(8,128)(2,1)} %param.14) | data formatting | bytes 7962624 | tf_op args[6]
  17.9 97.2 %shard_map.119 = (bf16[32,8,1152]{2,1,0:T(8,128)(2,1)}, f32[36,432]{1,0:T(8,128)}, f32[36,144]{1,0:T(8,128)}, f32[36,432]{1,0:T(8,128)}, f32[36,144]{1,0:T(8,128)}) custom-call(bf16[32,8,1152]{2,1,0:T(8,128)(2,1)} %bitcast.7, bf16[32,8,1152]{2,1,0:T(8,128)(2,1)} %bitcast.8, s32[32,8,1152]{2,1,0:T(8,128)} %bitcast.5, s32[32,8,1152]{2,1,0:T(8,128)} %bitcast.6, ...), custom_call_target="tpu_custom_call" | custom-call | tf_op jit(solution)/shard_map/pallas_call | solution.py:560
  115.1 0.0 copy-start.1
  115.2 0.0 copy-start.2
  115.2 2.0 %copy.22 = bf16[1,1,256,1152]{3,2,1,0:T(8,128)(2,1)} copy(bf16[1,1,256,1152]{3,2,1,0:T(8,128)(2,1)} %bitcast.9) | data formatting | bytes 1179648
  117.1 1.5 %copy.23 = f32[36,432]{1,0:T(8,128)} copy(f32[36,432]{1,0:T(8,128)} %get-tuple-element.21) | data formatting | bytes 124416
  118.7 1.4 %copy.24 = f32[36,144]{1,0:T(8,128)} copy(f32[36,144]{1,0:T(8,128)} %get-tuple-element.22) | data formatting | bytes 41472
  120.0 0.0 copy-done.1
  120.1 0.6 copy.25
  120.7 0.0 copy-done.2
  120.7 0.6 copy.26
Async XLA Ops:
  0.6 2.8 %copy-start = (bf16[1152,576]{0,1:T(8,128)(2,1)S(1)}, bf16[1152,576]{0,1:T(8,128)(2,1)}, u32[]{:S(2)}) copy-start(bf16[1152,576]{0,1:T(8,128)(2,1)} %param.15) | copy-start | bytes 3981316
  115.1 4.9 %copy-start.1 = (f32[36,432]{1,0:T(8,128)S(1)}, f32[36,432]{1,0:T(8,128)}, u32[]{:S(2)}) copy-start(f32[36,432]{1,0:T(8,128)} %get-tuple-element.23) | copy-start | bytes 186628
  115.2 5.5 %copy-start.2 = (f32[36,144]{1,0:T(8,128)S(1)}, f32[36,144]{1,0:T(8,128)}, u32[]{:S(2)}) copy-start(f32[36,144]{1,0:T(8,128)} %get-tuple-element.24) | copy-start | bytes 62212

commit v2 on v1

--- a/solution.py
+++ b/solution.py
@@ -35,10 +35,10 @@
     x=((32, 8, D), BF),
     ks=((32, 8, D), jnp.int32),
     kt=((32, 8, D), jnp.int32),
-    wqs=((D, 3 * INNER), BF),
-    wos=((D, INNER), BF),
-    wqt=((D, 3 * INNER), BF),
-    wot=((D, INNER), BF),
+    wqs=((3 * INNER, D), BF),
+    wos=((INNER, D), BF),
+    wqt=((3 * INNER, D), BF),
+    wot=((INNER, D), BF),
     go=((NS, 8, D), BF),
     y_out=((NS, 8, D), BF),
     y_in=((NS, 8, D), BF),
@@ -46,21 +46,19 @@
     d_in=((NS, 8, D), BF),
     normed_s=((T, D), BF),
     normed_t=((T, D), BF),
-    qkv=((T, 3 * INNER), BF),
-    hs_s=((24, T, 128), BF),
-    hs_t=((24, T, 128), BF),
+    hs_s=((24, HD, T), BF),
+    hs_t=((24, HD, T), BF),
     probs=((H, T, T), F32),
-    mh_s=((H, T, 128), BF),
-    mh_t=((H, T, 128), BF),
+    mh_s=((H, HD, T), BF),
+    mh_t=((H, HD, T), BF),
     mixed=((T, INNER), BF),
     dproj=((T, D), BF),
-    dmix=((T, INNER), BF),
-    dmh=((H, T, 128), BF),
-    dh=((24, T, 128), BF),
+    dmh=((H, HD, T), BF),
+    dh=((24, HD, T), BF),
     dqkv=((T, 3 * INNER), BF),
     dn=((T, D), F32),
-    dsel=((2, 2, T, D), BF),
-    dsel_in=((2, T, D), BF),
+    dsel=((2, 2, D, T), BF),
+    dsel_in=((2, D, T), BF),
     perm=((32 * RB, D), BF),
     lt=((2, 32 * RB, T), BF),
     lt_in=((2, 2, 32 * RB, T), BF),
@@ -198,53 +196,47 @@
 
         rows(fn)
 
-    def split_heads(src, dst, n):
-        for j in range(n):
-            v = src[:, HD * j: HD * (j + 1)]
-            dst[j] = jnp.concatenate([v, jnp.zeros((T, 128 - HD), BF)], axis=1)
+    def heads(ref, js):
+        return jnp.concatenate([ref[j].astype(F32) for j in js], axis=0)
 
     def qkv_heads(normed, w, hs):
-        for lo, hi in ((0, 512), (512, 1024), (1024, 1536), (1536, 1728)):
-            m.qkv[:, lo:hi] = nn(normed[...], w[:, lo:hi]).astype(BF)
-        split_heads(m.qkv, hs, 24)
+        for n in range(3):
+            part = nt(w[INNER * n: INNER * (n + 1), :], normed[...])
+            hs[H * n: H * (n + 1)] = part.reshape(H, HD, T).astype(BF)
 
     def d_proj_mix(dy, keep, wo):
         def fn(r, blk):
             m.dproj[r, :] = (flat(dy, blk) * (flat(keep, blk) * KEEP)).astype(BF)
 
         rows(fn)
-        m.dmix[...] = nn(m.dproj[...], wo[...]).astype(BF)
-        split_heads(m.dmix, m.dmh, H)
+        m.dmh[...] = nt(wo[...], m.dproj[...]).reshape(H, HD, T).astype(BF)
 
     def softmax(q, k, mask):
-        e = jnp.exp(nt(q, k) * SCALE)
+        e = jnp.exp(tn(q, k) * SCALE)
         if mask is not None:
             e = jnp.where(mask, e, 0.0)
-        return e / jnp.sum(e, axis=-1, keepdims=True)
+        return e * (1.0 / jnp.sum(e, axis=-1, keepdims=True))
 
     def attention_backward(h, p, p_low, q, k, v):
         dm = m.dmh[h]
-        dp_ = nt(dm, v)
+        dp_ = tn(dm, v)
         ds = (p * (dp_ - jnp.sum(p * dp_, axis=-1, keepdims=True)) * SCALE).astype(BF)
-        m.dh[h] = nn(ds, k).astype(BF)
-        m.dh[h + 8] = tn(ds, q).astype(BF)
-        m.dh[h + 16] = tn(p_low, dm).astype(BF)
+        m.dh[h] = nt(k, ds).astype(BF)
+        m.dh[h + 8] = nn(q, ds).astype(BF)
+        m.dh[h + 16] = nn(dm, p_low).astype(BF)
 
     def gather_columns(sec, mh):
-        for j in range(24):
-            m.dqkv[:, HD * j: HD * (j + 1)] = m.dh[j][:, :HD]
         for c in range(2):
-            for i in range(6):
-                m.dsel[sec, c, :, HD * i: HD * (i + 1)] = m.dh[6 * c + i][:, :HD]
-                lo = 432 + HD * i
-                m.dsel[sec, c, :, lo: lo + HD] = m.dh[12 + 6 * c + i][:, :HD]
-            for i, h in enumerate((2 * c, 2 * c + 1, 4 + 2 * c, 5 + 2 * c)):
-                lo = 864 + HD * i
-                m.dsel[sec, c, :, lo: lo + HD] = mh[h][:, :HD]
+            js = [6 * c + i for i in range(6)] + [12 + 6 * c + i for i in range(6)]
+            hs = (2 * c, 2 * c + 1, 4 + 2 * c, 5 + 2 * c)
+            both = jnp.concatenate([heads(m.dh, js), heads(mh, hs)], axis=0)
+            m.dsel[sec, c] = both.astype(BF)
 
     def input_backward(src, dy, dst, wq):
+        m.dqkv[:, 0:1152] = heads(m.dh, range(16)).T.astype(BF)
+        m.dqkv[:, 1152:1728] = heads(m.dh, range(16, 24)).T.astype(BF)
         for n in range(3):
-            m.dn[:, 384 * n: 384 * (n + 1)] = nt(m.dqkv[...], wq[384 * n: 384 * (n + 1), :])
+            m.dn[:, 384 * n: 384 * (n + 1)] = nn(m.dqkv[...], wq[:, 384 * n: 384 * (n + 1)])
 
         def fn(r, blk):
             zf = flat(src, blk)
@@ -286,8 +278,8 @@
         def step(n, carry):
             r = pl.ds(pl.multiple_of(n * 320, 320), 320)
             for i, lo, hi in ((0, 0, 384), (0, 384, 864), (1, 864, 1152)):
-                acc = nn(m.lt[i, r, :], m.dsel[sec, core, :, lo:hi])
-                acc = acc + nn(m.lt_in[sec, i, r, :], m.dsel_in[sec, :, lo:hi])
+                acc = nt(m.lt[i, r, :], m.dsel[sec, core, lo:hi, :])
+                acc = acc + nt(m.lt_in[sec, i, r, :], m.dsel_in[sec, lo:hi, :])
                 m.grad[sec, pl.ds(n * 2, 2), :, :, lo:hi] = acc.reshape(
                     2, 4, RB, hi - lo
                 ).astype(BF)
@@ -433,17 +425,16 @@
     def spatial_head(h, carry):
         p = softmax(m.hs_s[h], m.hs_s[h + 8], None)
         m.probs[h] = p
-        m.mh_s[h] = nn(p.astype(BF), m.hs_s[h + 16]).astype(BF)
+        m.mh_s[h] = nt(m.hs_s[h + 16], p.astype(BF)).astype(BF)
         return carry
 
     lax.fori_loop(0, H, spatial_head, 0)
-    for h in range(H):
-        m.mixed[:, HD * h: HD * (h + 1)] = m.mh_s[h][:, :HD]
+    m.mixed[...] = heads(m.mh_s, range(H)).T.astype(BF)
     loads[2].wait()
     loads[5].wait()
     for n in range(3):
         c = slice(384 * n, 384 * (n + 1))
-        proj = nt(m.mixed[...], m.wos[c, :]).reshape(32, 8, 384)
+        proj = nn(m.mixed[...], m.wos[:, c]).reshape(32, 8, 384)
         keep = m.ks[:, :, c].astype(F32) * KEEP
         m.y_out[:, :, c] = (m.x[:, :, c].astype(F32) + proj * keep).astype(BF)
     a2a_start(1, m.y_out, m.y_in)
@@ -485,7 +476,7 @@
         q, k, v = m.hs_t[h], m.hs_t[h + 8], m.hs_t[h + 16]
         p = softmax(q, k, mask)
         p_low = p.astype(BF)
-        m.mh_t[h] = nn(p_low, v).astype(BF)
+        m.mh_t[h] = nt(v, p_low).astype(BF)
         attention_backward(h, p, p_low, q, k, v)
         return carry
 
@@ -543,6 +534,15 @@
     reduce_drain(0)
     reduce_drain(1)
     store.wait()
+
+
+def hand_over(*refs):
+    sem = refs[10]
+    copies = [pltpu.make_async_copy(refs[i], refs[5 + i], sem.at[i]) for i in range(5)]
+    for c in copies:
+        c.start()
+    for c in copies:
+        c.wait()
 
 
 def shards(
@@ -578,11 +578,18 @@
         out_grad.reshape(32, 8, D),
         spatial_keep.reshape(32, 8, D),
         temporal_keep.reshape(32, 8, D),
-        spatial_qkv,
-        spatial_out,
-        temporal_qkv,
-        temporal_out,
+        spatial_qkv.T,
+        spatial_out.T,
+        temporal_qkv.T,
+        temporal_out.T,
     )
+    outs = pl.pallas_call(
+        hand_over,
+        out_shape=tuple(jax.ShapeDtypeStruct(o.shape, o.dtype) for o in outs),
+        in_specs=[vmem] * 5,
+        out_specs=(hbm,) * 5,
+        scratch_shapes=[pltpu.SemaphoreType.DMA((5,))],
+    )(*outs)
     return (outs[0].reshape(1, 1, T, D),) + tuple(outs[1:])
 
 

time: 122 us -> 96.1 us (0.79)
  local copies, waits for them, and re-layouts: 23.4 us -> 0 us
  Pallas kernels: 97.2 us -> 95.3 us
    unnamed x15 -> x0, local copies, waits for them, and re-layouts: 23.4 us -> none
    pallas_call x1, Pallas kernels: 97.2 us -> 93.2 us  [shards(): pl.pallas_call(body, out_shape=(jax.ShapeDtypeStruct((32, 8, D), BF), jax...]
    pallas_call x0 -> x1, Pallas kernels: none -> 2.08 us  [shards(): pl.pallas_call(hand_over, out_shape=tuple((jax.ShapeDtypeStruct(o.shape,...]
where the time goes in v2:
time: 96.1 us; the launch traced here: 95.9 us
  Pallas kernels  95.3 us (99%)
    pallas_call x1, Pallas kernels, shards(): pl.pallas_call(body, out_shape=(jax.ShapeDtypeStruct((32, 8, D), BF), jax...  93.2 us
    pallas_call x1, Pallas kernels, shards(): pl.pallas_call(hand_over, out_shape=tuple((jax.ShapeDtypeStruct(o.shape,...  2.08 us

profile of v2, /device:TPU:0, one launch (start us, length us, event | category | flops | bytes accessed | tf_op | source)
XLA Modules:
  0.0 95.9 jit_solution(14266264451112738209)
XLA Ops:
  0.6 93.2 %shard_map.119 = (bf16[32,8,1152]{2,1,0:T(8,128)(2,1)}, f32[36,432]{1,0:T(8,128)}, f32[36,144]{1,0:T(8,128)}, f32[36,432]{1,0:T(8,128)}, f32[36,144]{1,0:T(8,128)}) custom-call(bf16[32,8,1152]{2,1,0:T(8,128)(2,1)} %bitcast.15, bf16[32,8,1152]{2,1,0:T(8,128)(2,1)} %bitcast.16, s32[32,8,1152]{2,1,0:T(8,128)} %bitcast.13, s32[32,8,1152]{2,1,0:T(8,128)} %bitcast.14, ...), custom_call_target="tpu_custom_call" | custom-call | tf_op jit(solution)/shard_map/pallas_call | solution.py:560
  93.9 2.1 %shard_map.120 = (bf16[32,8,1152]{2,1,0:T(8,128)(2,1)}, f32[36,432]{1,0:T(8,128)}, f32[36,144]{1,0:T(8,128)}, f32[36,432]{1,0:T(8,128)}, f32[36,144]{1,0:T(8,128)}) custom-call(bf16[32,8,1152]{2,1,0:T(8,128)(2,1)} %get-tuple-element.15.refs_0_, f32[36,432]{1,0:T(8,128)} %get-tuple-element.16.refs_1_, f32[36,144]{1,0:T(8,128)} %get-tuple-element.17.refs_2_, ...), custom_call_target="tpu_custom_call" | custom-call | tf_op jit(solution)/shard_map/pallas_call | solution.py:586

commit v3 on v2

--- a/solution.py
+++ b/solution.py
@@ -60,15 +60,8 @@
     dsel=((2, 2, D, T), BF),
     dsel_in=((2, D, T), BF),
     perm=((32 * RB, D), BF),
-    lt=((2, 32 * RB, T), BF),
+    lt=((2, 2, 32 * RB, T), BF),
     lt_in=((2, 2, 32 * RB, T), BF),
-    grad=((2, 8, 4, RB, D), BF),
-    r1=((2, 2, 2, 2, RB, D), BF),
-    r2=((2, 2, 2, 4, RB, D), BF),
-    hsum=((2, 2, 4, RB, D), BF),
-    r3=((2, 2, 3, RB, D), BF),
-    zsum=((2, 2, 2, RB, INNER), BF),
-    r4=((2, 3, RB, INNER), BF),
     dx=((32, 8, D), BF),
 )
 SEMS = dict(
@@ -76,17 +69,32 @@
     store=(1,),
     a2a_s=(3, 31),
     a2a_r=(3, 31),
-    core_s=(2, 3),
-    core_r=(2, 3),
-    r1_s=(2, 2, 2),
-    r1_r=(2, 2, 2),
-    r2_s=(2, 2, 2, 2),
-    r2_r=(2, 2, 2, 2),
-    r3_s=(2, 2, 3),
-    r3_r=(2, 2, 3),
-    r4_s=(2, 3),
-    r4_r=(2, 3),
+    core_s=(2, 4),
+    core_r=(2, 4),
 )
+BATCHES = dict(time=(896, 512, True), out=(384, 256, False), space=(640, 384, True))
+for _n, (_w, _z, _c) in BATCHES.items():
+    SCRATCH.update({
+        _n + "_g": ((8, 4, RB, _w), BF),
+        _n + "_r1": ((2, 2, 2, RB, _w), BF),
+        _n + "_r2": ((2, 2, 4, RB, _w), BF),
+        _n + "_h": ((2, 4, RB, _w), BF),
+        _n + "_r3": ((2, 3, RB, _w), BF),
+        _n + "_z": ((2, 2, RB, _z), BF),
+        _n + "_r4": ((3, RB, _z), BF),
+    })
+    SEMS.update({
+        _n + "_r1_s": (2, 2), _n + "_r1_r": (2, 2), _n + "_r2_s": (2, 2, 2), _n + "_r2_r": (2, 2, 2),
+        _n + "_r3_s": (2, 3), _n + "_r3_r": (2, 3), _n + "_r4_s": (3,), _n + "_r4_r": (3,),
+    })
+    if _c:
+        SCRATCH.update({
+            _n + "_c": ((2, 2, 4, 4, RB, 128), BF),
+            _n + "_ci": ((3, 4, 4, RB, 128), BF),
+            _n + "_cs": ((4, 4, RB, 128), BF),
+            _n + "_cj": ((15, RB, 128), BF),
+        })
+        SEMS.update({_n + "_ci_s": (3,), _n + "_ci_r": (3,), _n + "_cj_s": (15,), _n + "_cj_r": (15,)})
 
 
 class Refs:
@@ -225,12 +233,17 @@
         m.dh[h + 8] = nn(q, ds).astype(BF)
         m.dh[h + 16] = nn(dm, p_low).astype(BF)
 
-    def gather_columns(sec, mh):
+    def gather_columns(sec):
         for c in range(2):
-            js = [6 * c + i for i in range(6)] + [12 + 6 * c + i for i in range(6)]
+            z0 = heads(m.dh, [6 * c + i for i in range(6)])
+            z1 = heads(m.dh, [12 + 6 * c + i for i in range(6)])
+            parts = [z0[:128], z1[:128], z0[128:], z1[128:]]
+            m.dsel[sec, c, 0:864] = jnp.concatenate(parts, axis=0).astype(BF)
+
+    def gather_mixed(sec, mh):
+        for c in range(2):
             hs = (2 * c, 2 * c + 1, 4 + 2 * c, 5 + 2 * c)
-            both = jnp.concatenate([heads(m.dh, js), heads(mh, hs)], axis=0)
-            m.dsel[sec, c] = both.astype(BF)
+            m.dsel[sec, c, 864:1152] = heads(mh, hs).astype(BF)
 
     def input_backward(src, dy, dst, wq):
         m.dqkv[:, 0:1152] = heads(m.dh, range(16)).T.astype(BF)
@@ -250,9 +263,10 @@
 
     def core_copies(sec):
         pairs = (
-            (m.lt.at[0], m.lt_in.at[sec, 0]),
-            (m.lt.at[1], m.lt_in.at[sec, 1]),
-            (m.dsel.at[sec, 1 - core], m.dsel_in.at[sec]),
+            (m.lt.at[sec, 0], m.lt_in.at[sec, 0]),
+            (m.lt.at[sec, 1], m.lt_in.at[sec, 1]),
+            (m.dsel.at[sec, 1 - core, 0:864], m.dsel_in.at[sec, 0:864]),
+            (m.dsel.at[sec, 1 - core, 864:1152], m.dsel_in.at[sec, 864:1152]),
         )
         return [
             pltpu.make_async_remote_copy(
@@ -266,26 +280,49 @@
             for i, (src, dst) in enumerate(pairs)
         ]
 
-    def transpose_rows(i, src):
+    def transpose_rows(sec, i, src):
         def step(n, carry):
             r = pl.ds(pl.multiple_of(n * 320, 320), 320)
-            m.lt[i, r, :] = nt(m.perm[r, :], src[...]).astype(BF)
+            m.lt[sec, i, r, :] = nt(m.perm[r, :], src[...]).astype(BF)
             return carry
 
         lax.fori_loop(0, 4, step, 0)
 
-    def weight_grads(sec):
-        def step(n, carry):
-            r = pl.ds(pl.multiple_of(n * 320, 320), 320)
-            for i, lo, hi in ((0, 0, 384), (0, 384, 864), (1, 864, 1152)):
-                acc = nt(m.lt[i, r, :], m.dsel[sec, core, lo:hi, :])
-                acc = acc + nt(m.lt_in[sec, i, r, :], m.dsel_in[sec, lo:hi, :])
-                m.grad[sec, pl.ds(n * 2, 2), :, :, lo:hi] = acc.reshape(
-                    2, 4, RB, hi - lo
-                ).astype(BF)
-            return carry
-
-        lax.fori_loop(0, 4, step, 0)
+    def grad_of(sec, i, o, lo, hi):
+        r = slice(640 * o, 640 * (o + 1))
+        acc = nt(m.lt[sec, i, r, :], m.dsel[sec, core, lo:hi, :])
+        acc = acc + nt(m.lt_in[sec, i, r, :], m.dsel_in[sec, lo:hi, :])
+        return acc
+
+    def widen(acc, width):
+        return jnp.concatenate([acc, jnp.zeros((acc.shape[0], width - acc.shape[1]), F32)], axis=1)
+
+    def blocks(acc):
+        return acc.reshape(4, 4, RB, acc.shape[1]).astype(BF)
+
+    def grad_first(sec, n):
+        dst = getattr(m, n + "_c")
+        for o in range(2):
+            acc = grad_of(sec, 0, o, 0, 256)
+            dst[0, o] = blocks(acc[:, :128])
+            dst[1, o] = blocks(acc[:, 128:])
+
+    def grad_rest(sec, n):
+        dst = getattr(m, n + "_g")
+        for o in range(2):
+            acc = grad_of(sec, 0, o, 256, 864)
+            if n == "space":
+                acc = widen(acc, 640)
+            dst[4 * o: 4 * o + 4, :, :, 0: acc.shape[1]] = blocks(acc)
+
+    def grad_out(sec, n):
+        dst = getattr(m, n + "_g")
+        for o in range(2):
+            acc = grad_of(sec, 1, o, 864, 1152)
+            if n == "out":
+                dst[4 * o: 4 * o + 4] = blocks(widen(acc, 384))
+            else:
+                dst[4 * o: 4 * o + 4, :, :, 608:896] = blocks(acc)
 
     def ring(o):
         return cx if o == 0 else cy
@@ -301,126 +338,184 @@
             src_ref=src, dst_ref=dst, send_sem=ssem, recv_sem=rsem, device_id=to, device_id_type=MESH
         )
 
-    def first_copies(sec, o):
-        i = ring(o)
-        up, dn, opp = lax.rem(i + 1, 4), lax.rem(i + 3, 4), lax.rem(i + 2, 4)
-        g = m.grad
-        one = [
-            remote(g.at[sec, o * 4 + opp, 0:2], m.r1.at[sec, o, 0],
-                   m.r1_s_sem.at[sec, o, 0], m.r1_r_sem.at[sec, o, 0], on_first(o, up)),
-            remote(g.at[sec, o * 4 + opp, 2:4], m.r1.at[sec, o, 1],
-                   m.r1_s_sem.at[sec, o, 1], m.r1_r_sem.at[sec, o, 1], on_first(o, dn)),
-        ]
-        two = [
-            [
-                remote(g.at[sec, o * 4 + up, 2 * b: 2 * b + 2], m.r2.at[sec, o, 0, 2 * b: 2 * b + 2],
-                       m.r2_s_sem.at[sec, o, 0, b], m.r2_r_sem.at[sec, o, 0, b], on_first(o, up))
-                for b in range(2)
-            ],
-            [
-                remote(g.at[sec, o * 4 + dn, 2 * b: 2 * b + 2], m.r2.at[sec, o, 1, 2 * b: 2 * b + 2],
-                       m.r2_s_sem.at[sec, o, 1, b], m.r2_r_sem.at[sec, o, 1, b], on_first(o, dn))
-                for b in range(2)
-            ],
-        ]
-        return one, two, up, dn, i
-
-    def reduce_start(sec):
-        for o in range(2):
-            one, two, up, dn, i = first_copies(sec, o)
-            one[0].start()
-            one[1].start()
-            two[0][1].start()
-            two[1][0].start()
-
-    def reduce_relay(sec):
-        for o in range(2):
-            one, two, up, dn, i = first_copies(sec, o)
-            for side, chunk, b in ((0, up, 0), (1, dn, 1)):
-                one[side].wait_recv()
-                for e in range(2 * b, 2 * b + 2):
-                    acc = m.grad[sec, o * 4 + chunk, e].astype(F32)
-                    acc = acc + m.r1[sec, o, side, e - 2 * b].astype(F32)
-                    m.grad[sec, o * 4 + chunk, e] = acc.astype(BF)
-                two[side][b].start()
-
-    def second_copies(sec, o):
-        j = ring(1 - o)
-        return [
-            remote(m.hsum.at[sec, o, lax.rem(j + d, 4)], m.r3.at[sec, o, d - 1],
-                   m.r3_s_sem.at[sec, o, d - 1], m.r3_r_sem.at[sec, o, d - 1],
-                   on_second(o, lax.rem(j + d, 4)))
-            for d in (1, 2, 3)
-        ]
-
-    def reduce_second(sec):
-        for o in range(2):
-            one, two, up, dn, i = first_copies(sec, o)
-            for side in two:
-                for c in side:
+    class Batch:
+        def __init__(self, n):
+            self.n = n
+            for k in ("g", "r1", "r2", "h", "r3", "z", "r4", "c", "ci", "cs", "cj"):
+                setattr(self, k, getattr(m, n + "_" + k, None))
+            for k in ("r1", "r2", "r3", "r4", "ci", "cj"):
+                for side in "sr":
+                    name = k + "_" + side
+                    setattr(self, name, getattr(m, n + "_" + name + "_sem", None))
+
+        def first(self, o):
+            i = ring(o)
+            up, dn, opp = lax.rem(i + 1, 4), lax.rem(i + 3, 4), lax.rem(i + 2, 4)
+            one = [
+                remote(self.g.at[o * 4 + opp, 2 * k: 2 * k + 2], self.r1.at[o, k],
+                       self.r1_s.at[o, k], self.r1_r.at[o, k], on_first(o, to))
+                for k, to in ((0, up), (1, dn))
+            ]
+            two = [
+                [
+                    remote(self.g.at[o * 4 + to, 2 * b: 2 * b + 2], self.r2.at[o, k, 2 * b: 2 * b + 2],
+                           self.r2_s.at[o, k, b], self.r2_r.at[o, k, b], on_first(o, to))
+                    for b in range(2)
+                ]
+                for k, to in ((0, up), (1, dn))
+            ]
+            return one, two, up, dn, i
+
+        def start(self):
+            firsts = [self.first(o) for o in range(2)]
+            for one, two, up, dn, i in firsts:
+                one[0].start()
+                one[1].start()
+            for one, two, up, dn, i in firsts:
+                two[0][1].start()
+                two[1][0].start()
+
+        def relay(self):
+            for o in range(2):
+                one, two, up, dn, i = self.first(o)
+                for side, chunk, b in ((0, up, 0), (1, dn, 1)):
+                    one[side].wait_recv()
+                    for e in range(2):
+                        acc = self.g[o * 4 + chunk, 2 * b + e].astype(F32)
+                        acc = acc + self.r1[o, side, e].astype(F32)
+                        self.g[o * 4 + chunk, 2 * b + e] = acc.astype(BF)
+                    two[side][b].start()
+
+        def second_copies(self, o):
+            j = ring(1 - o)
+            return [
+                remote(self.h.at[o, lax.rem(j + d, 4)], self.r3.at[o, d - 1],
+                       self.r3_s.at[o, d - 1], self.r3_r.at[o, d - 1],
+                       on_second(o, lax.rem(j + d, 4)))
+                for d in (1, 2, 3)
+            ]
+
+        def second(self):
+            for o in range(2):
+                one, two, up, dn, i = self.first(o)
+                for side in two:
+                    for c in side:
+                        c.wait_recv()
+                for e in range(4):
+                    acc = self.g[o * 4 + i, e].astype(F32)
+                    acc = acc + self.r2[o, 0, e].astype(F32)
+                    acc = acc + self.r2[o, 1, e].astype(F32)
+                    self.h[o, e] = acc.astype(BF)
+                for c in self.second_copies(o):
+                    c.start()
+
+        def z_copies(self):
+            copies = []
+            for d in (1, 2, 3):
+                z = lax.rem(cz + d, 4)
+                copies.append(
+                    remote(self.z.at[lax.rem(z, 2), z // 2], self.r4.at[d - 1],
+                           self.r4_s.at[d - 1], self.r4_r.at[d - 1], place(cx, cy, z))
+                )
+            return copies
+
+        def third(self):
+            for o in range(2):
+                for c in self.second_copies(o):
                     c.wait_recv()
-            for e in range(4):
-                acc = m.grad[sec, o * 4 + i, e].astype(F32)
-                acc = acc + m.r2[sec, o, 0, e].astype(F32)
-                acc = acc + m.r2[sec, o, 1, e].astype(F32)
-                m.hsum[sec, o, e] = acc.astype(BF)
-            for c in second_copies(sec, o):
+                acc = self.h[o, ring(1 - o)].astype(F32)
+                for d in range(3):
+                    acc = acc + self.r3[o, d].astype(F32)
+                for z in range(2):
+                    if self.n == "out":
+                        v = acc[:, 144 * z: 144 * (z + 1)]
+                    else:
+                        v = acc[:, 304 * z: 304 * (z + 1)]
+                    if self.n == "time":
+                        low = 608 + 144 * z
+                        v = jnp.concatenate([v, acc[:, low: low + 144]], axis=1)
+                    self.z[o, z] = widen(v, BATCHES[self.n][1]).astype(BF)
+            for c in self.z_copies():
                 c.start()
 
-    def z_copies(sec):
-        copies = []
-        for d in (1, 2, 3):
-            z = lax.rem(cz + d, 4)
-            copies.append(
-                remote(m.zsum.at[sec, lax.rem(z, 2), z // 2], m.r4.at[sec, d - 1],
-                       m.r4_s_sem.at[sec, d - 1], m.r4_r_sem.at[sec, d - 1], place(cx, cy, z))
-            )
-        return copies
-
-    def reduce_z(sec):
-        for o in range(2):
-            for c in second_copies(sec, o):
+        def ci_copies(self):
+            copies = []
+            for d in (1, 2, 3):
+                z = lax.rem(cz + d, 4)
+                copies.append(
+                    remote(self.c.at[z // 2, lax.rem(z, 2)], self.ci.at[d - 1],
+                           self.ci_s.at[d - 1], self.ci_r.at[d - 1], place(cx, cy, z))
+                )
+            return copies
+
+        def cj_copies(self):
+            copies = []
+            for d in range(1, 16):
+                x, y = lax.rem(cx + d // 4, 4), lax.rem(cy + d % 4, 4)
+                a, b = x * (1 - zl) + y * zl, y * (1 - zl) + x * zl
+                copies.append(
+                    remote(self.cs.at[a, b], self.cj.at[d - 1],
+                           self.cj_s.at[d - 1], self.cj_r.at[d - 1], place(x, y, cz))
+                )
+            return copies
+
+        def c_start(self):
+            for c in self.ci_copies():
+                c.start()
+
+        def c_second(self):
+            for c in self.ci_copies():
                 c.wait_recv()
-            acc = m.hsum[sec, o, ring(1 - o)].astype(F32)
+
+            def add(a, carry):
+                acc = self.c[zh, zl, a].astype(F32)
+                for d in range(3):
+                    acc = acc + self.ci[d, a].astype(F32)
+                self.cs[a] = acc.astype(BF)
+                return carry
+
+            lax.fori_loop(0, 4, add, 0)
+            for c in self.cj_copies():
+                c.start()
+
+        def c_end(self):
+            for c in self.cj_copies():
+                c.wait_recv()
+            a, b = cx * (1 - zl) + cy * zl, cy * (1 - zl) + cx * zl
+            acc = self.cs[a, b].astype(F32)
+            for d in range(15):
+                acc = acc + self.cj[d].astype(F32)
+            return acc
+
+        def end(self):
+            for c in self.z_copies():
+                c.wait_recv()
+            acc = self.z[zl, zh].astype(F32)
             for d in range(3):
-                acc = acc + m.r3[sec, o, d].astype(F32)
-            for z in range(2):
-                m.zsum[sec, o, z] = jnp.concatenate(
-                    [acc[:, 432 * z: 432 * (z + 1)], acc[:, 864 + 144 * z: 864 + 144 * (z + 1)]],
-                    axis=1,
-                ).astype(BF)
-        for c in z_copies(sec):
-            c.start()
-
-    def reduce_end(sec, gq, gout):
-        for c in z_copies(sec):
-            c.wait_recv()
-        acc = m.zsum[sec, zl, zh].astype(F32)
-        for d in range(3):
-            acc = acc + m.r4[sec, d].astype(F32)
-        gq[...] = acc[0:36, 0:432]
-        gout[...] = acc[0:36, 432:576]
-
-    def reduce_drain(sec):
-        for c in core_copies(sec)[2:]:
-            c.wait_send()
-        for o in range(2):
-            one, two, up, dn, i = first_copies(sec, o)
-            for c in one + two[0] + two[1]:
+                acc = acc + self.r4[d].astype(F32)
+            return acc
+
+        def drain(self):
+            for o in range(2):
+                one, two, up, dn, i = self.first(o)
+                for c in one + two[0] + two[1] + self.second_copies(o):
+                    c.wait_send()
+            for c in self.z_copies():
                 c.wait_send()
-            for c in second_copies(sec, o):
-                c.wait_send()
-        for c in z_copies(sec):
-            c.wait_send()
+            if self.c is not None:
+                for c in self.ci_copies() + self.cj_copies():
+                    c.wait_send()
+
+    b_time, b_out, b_space = Batch("time"), Batch("out"), Batch("space")
 
     loads[0].wait()
     normalize(m.x, m.normed_s)
+    loads[4].wait()
+    qkv_heads(m.normed_s, m.wqs, m.hs_s)
     pl.semaphore_wait(barrier, NS + 2)
     a2a_start(0, ins[1], m.go)
     own = pltpu.make_async_copy(ins[1].at[me], m.go.at[me], m.load_sem.at[1])
     own.start()
-    loads[4].wait()
-    qkv_heads(m.normed_s, m.wqs, m.hs_s)
 
     def spatial_head(h, carry):
         p = softmax(m.hs_s[h], m.hs_s[h + 8], None)
@@ -456,14 +551,18 @@
         return carry
 
     lax.fori_loop(0, NS // 2, perm_step, 0)
+    gather_mixed(1, m.mh_s)
+    core_copies(1)[3].start()
 
     own.wait()
     a2a_wait(0, m.go, m.go)
     loads[3].wait()
     loads[7].wait()
     d_proj_mix(m.go, m.kt, m.wot)
-    transpose_rows(1, m.dproj)
+    transpose_rows(0, 1, m.dproj)
     core_copies(0)[1].start()
+    transpose_rows(1, 0, m.normed_s)
+    core_copies(1)[0].start()
     a2a_wait(1, m.y_out, m.y_in)
     normalize(m.y_in, m.normed_t)
     loads[6].wait()
@@ -481,27 +580,28 @@
         return carry
 
     lax.fori_loop(0, H, temporal_head, 0)
-    gather_columns(0, m.mh_t)
-    core_copies(0)[2].start()
     input_backward(m.y_in, m.go, m.d_out, m.wqt)
     a2a_start(2, m.d_out, m.d_in)
     m.d_in[me] = m.d_out[me]
-    transpose_rows(0, m.normed_t)
+    gather_columns(0)
+    gather_mixed(0, m.mh_t)
+    core_copies(0)[2].start()
+    core_copies(0)[3].start()
+    transpose_rows(0, 0, m.normed_t)
     core_copies(0)[0].start()
     for c in core_copies(0):
         c.wait_recv()
-    weight_grads(0)
-    for c in core_copies(0)[:2]:
-        c.wait_send()
-
-    transpose_rows(0, m.normed_s)
-    core_copies(1)[0].start()
+    grad_first(0, "time")
+    b_time.c_start()
+    grad_rest(0, "time")
+    grad_out(0, "time")
+    b_time.start()
+
     a2a_wait(2, m.d_out, m.d_in)
-    reduce_start(0)
     d_proj_mix(m.d_in, m.ks, m.wos)
-    transpose_rows(1, m.dproj)
+    transpose_rows(1, 1, m.dproj)
     core_copies(1)[1].start()
-    reduce_relay(0)
+    b_time.relay()
 
     def spatial_back(h, carry):
         p = m.probs[h]
@@ -509,30 +609,48 @@
         return carry
 
     lax.fori_loop(0, H, spatial_back, 0)
-    gather_columns(1, m.mh_s)
+    gather_columns(1)
     core_copies(1)[2].start()
-    reduce_second(0)
-    for c in core_copies(1):
-        c.wait_recv()
-    weight_grads(1)
-    reduce_start(1)
-    reduce_z(0)
+    core_copies(1)[1].wait_recv()
+    core_copies(1)[3].wait_recv()
+    grad_out(1, "out")
+    b_out.start()
+    core_copies(1)[0].wait_recv()
+    core_copies(1)[2].wait_recv()
+    grad_first(1, "space")
+    b_space.c_start()
+    grad_rest(1, "space")
+    b_space.start()
+    b_time.second()
+    b_time.c_second()
+    b_out.relay()
     input_backward(m.x, m.d_in, m.dx, m.wqs)
     store = pltpu.make_async_copy(m.dx, dx_hbm, m.store_sem.at[0])
     store.start()
-    reduce_end(0, gqt, got)
-    reduce_relay(1)
-    reduce_second(1)
-    reduce_z(1)
-    reduce_end(1, gqs, gos)
+    b_space.relay()
+    b_space.c_second()
+    b_time.third()
+    b_out.second()
+    b_space.second()
+    first = b_time.c_end()
+    rest = b_time.end()
+    gqt[...] = jnp.concatenate([first[0:36], rest[0:36, 0:304]], axis=1)
+    got[...] = rest[0:36, 304:448]
+    b_out.third()
+    b_space.third()
+    first = b_space.c_end()
+    gos[...] = b_out.end()[0:36, 0:144]
+    rest = b_space.end()
+    gqs[...] = jnp.concatenate([first[0:36], rest[0:36, 0:304]], axis=1)
 
     a2a_drain(0, ins[1], m.go)
     a2a_drain(1, m.y_out, m.y_in)
     a2a_drain(2, m.d_out, m.d_in)
-    for c in core_copies(1)[:2]:
+    for c in core_copies(0) + core_copies(1):
         c.wait_send()
-    reduce_drain(0)
-    reduce_drain(1)
+    b_time.drain()
+    b_out.drain()
+    b_space.drain()
     store.wait()
 
 

time: 96.1 us -> 90.6 us (0.943)
  Pallas kernels: 95.3 us -> 89.6 us
    pallas_call x1, Pallas kernels: 93.2 us -> 87.5 us  [shards(): pl.pallas_call(body, out_shape=(jax.ShapeDtypeStruct((32, 8, D), BF), jax...]
where the time goes in v3:
time: 90.6 us; the launch traced here: 90.4 us
  Pallas kernels  89.6 us (99%)
    pallas_call x1, Pallas kernels, shards(): pl.pallas_call(body, out_shape=(jax.ShapeDtypeStruct((32, 8, D), BF), jax...  87.5 us
    pallas_call x1, Pallas kernels, shards(): pl.pallas_call(hand_over, out_shape=tuple((jax.ShapeDtypeStruct(o.shape,...  2.08 us

profile of v3, /device:TPU:0, one launch (start us, length us, event | category | flops | bytes accessed | tf_op | source)
XLA Modules:
  0.0 90.4 jit_solution(6024536079733926011)
XLA Ops:
  0.6 87.5 %shard_map.119 = (bf16[32,8,1152]{2,1,0:T(8,128)(2,1)}, f32[36,432]{1,0:T(8,128)}, f32[36,144]{1,0:T(8,128)}, f32[36,432]{1,0:T(8,128)}, f32[36,144]{1,0:T(8,128)}) custom-call(bf16[32,8,1152]{2,1,0:T(8,128)(2,1)} %bitcast.15, bf16[32,8,1152]{2,1,0:T(8,128)(2,1)} %bitcast.16, s32[32,8,1152]{2,1,0:T(8,128)} %bitcast.13, s32[32,8,1152]{2,1,0:T(8,128)} %bitcast.14, ...), custom_call_target="tpu_custom_call" | custom-call | tf_op jit(solution)/shard_map/pallas_call | solution.py:678
  88.2 2.1 %shard_map.120 = (bf16[32,8,1152]{2,1,0:T(8,128)(2,1)}, f32[36,432]{1,0:T(8,128)}, f32[36,144]{1,0:T(8,128)}, f32[36,432]{1,0:T(8,128)}, f32[36,144]{1,0:T(8,128)}) custom-call(bf16[32,8,1152]{2,1,0:T(8,128)(2,1)} %get-tuple-element.15.refs_0_, f32[36,432]{1,0:T(8,128)} %get-tuple-element.16.refs_1_, f32[36,144]{1,0:T(8,128)} %get-tuple-element.17.refs_2_, ...), custom_call_target="tpu_custom_call" | custom-call | tf_op jit(solution)/shard_map/pallas_call | solution.py:704

commit v4 on v3

--- a/solution.py
+++ b/solution.py
@@ -12,6 +12,8 @@
 T = 256
 NS = 32
 RB = 40
+PB = 72
+HEADS_AT_ONCE = 4
 MESH = pl.DeviceIdType.MESH
 BF = jnp.bfloat16
 F32 = jnp.float32
@@ -59,9 +61,9 @@
     dn=((T, D), F32),
     dsel=((2, 2, D, T), BF),
     dsel_in=((2, D, T), BF),
-    perm=((32 * RB, D), BF),
-    lt=((2, 2, 32 * RB, T), BF),
-    lt_in=((2, 2, 32 * RB, T), BF),
+    perm=((D, D), BF),
+    lt=((2, 2, D, T), BF),
+    lt_in=((2, 2, D, T), BF),
     dx=((32, 8, D), BF),
 )
 SEMS = dict(
@@ -75,9 +77,9 @@
 BATCHES = dict(time=(896, 512, True), out=(384, 256, False), space=(640, 384, True))
 for _n, (_w, _z, _c) in BATCHES.items():
     SCRATCH.update({
-        _n + "_g": ((8, 4, RB, _w), BF),
-        _n + "_r1": ((2, 2, 2, RB, _w), BF),
-        _n + "_r2": ((2, 2, 4, RB, _w), BF),
+        _n + "_g": ((8, 2, PB, _w), BF),
+        _n + "_r1": ((2, 2, PB, _w), BF),
+        _n + "_r2": ((2, 2, 2, PB, _w), BF),
         _n + "_h": ((2, 4, RB, _w), BF),
         _n + "_r3": ((2, 3, RB, _w), BF),
         _n + "_z": ((2, 2, RB, _z), BF),
@@ -89,8 +91,8 @@
     })
     if _c:
         SCRATCH.update({
-            _n + "_c": ((2, 2, 4, 4, RB, 128), BF),
-            _n + "_ci": ((3, 4, 4, RB, 128), BF),
+            _n + "_c": ((2, 2, 4, 2, PB, 128), BF),
+            _n + "_ci": ((3, 4, 2, PB, 128), BF),
             _n + "_cs": ((4, 4, RB, 128), BF),
             _n + "_cj": ((15, RB, 128), BF),
         })
@@ -124,8 +126,8 @@
         None if dst is None else pltpu.make_async_copy(src, dst, m.load_sem.at[i])
         for i, (src, dst) in enumerate(zip(ins, dests))
     ]
-    for i in (0, 4, 2, 5, 7, 3, 6):
-        loads[i].start()
+    loads[0].start()
+    loads[4].start()
 
     barrier = pltpu.get_barrier_semaphore()
 
@@ -161,6 +163,13 @@
             return carry
 
         lax.fori_loop(1, NS, step, 0)
+
+    def a2a_send(k, src, dst, to):
+        d = lax.rem(to - me + NS, NS)
+
+        @pl.when(d != 0)
+        def _():
+            a2a_copy(k, src, dst, d).start()
 
     def a2a_wait(k, src, dst):
         def step(d, carry):
@@ -184,9 +193,12 @@
 
         lax.fori_loop(1, NS, step, 0)
 
-    def rows(fn):
-        def step(r, carry):
+    def rows(fn, first=0, then=None):
+        def step(i, carry):
+            r = lax.rem(i + first, 8)
             fn(pl.ds(pl.multiple_of(r * 32, 32), 32), pl.ds(r * 4, 4))
+            if then is not None:
+                then(r)
             return carry
 
         lax.fori_loop(0, 8, step, 0)
@@ -218,6 +230,14 @@
 
         rows(fn)
         m.dmh[...] = nt(wo[...], m.dproj[...]).reshape(H, HD, T).astype(BF)
+
+    def some_heads(lo, hi, fn):
+        def step(i, carry):
+            for j in range(HEADS_AT_ONCE):
+                fn(i * HEADS_AT_ONCE + j)
+            return carry
+
+        lax.fori_loop(lo // HEADS_AT_ONCE, hi // HEADS_AT_ONCE, step, 0)
 
     def softmax(q, k, mask):
         e = jnp.exp(tn(q, k) * SCALE)
@@ -245,7 +265,7 @@
             hs = (2 * c, 2 * c + 1, 4 + 2 * c, 5 + 2 * c)
             m.dsel[sec, c, 864:1152] = heads(mh, hs).astype(BF)
 
-    def input_backward(src, dy, dst, wq):
+    def input_backward(src, dy, dst, wq, then=None):
         m.dqkv[:, 0:1152] = heads(m.dh, range(16)).T.astype(BF)
         m.dqkv[:, 1152:1728] = heads(m.dh, range(16, 24)).T.astype(BF)
         for n in range(3):
@@ -259,7 +279,7 @@
             dz = flat(dy, blk) + inv * (dn - c * jnp.mean(dn * c, axis=-1, keepdims=True))
             dst[blk] = dz.reshape(4, 8, D).astype(BF)
 
-        rows(fn)
+        rows(fn, me // 4, then)
 
     def core_copies(sec):
         pairs = (
@@ -282,14 +302,14 @@
 
     def transpose_rows(sec, i, src):
         def step(n, carry):
-            r = pl.ds(pl.multiple_of(n * 320, 320), 320)
+            r = pl.ds(pl.multiple_of(n * 288, 288), 288)
             m.lt[sec, i, r, :] = nt(m.perm[r, :], src[...]).astype(BF)
             return carry
 
         lax.fori_loop(0, 4, step, 0)
 
     def grad_of(sec, i, o, lo, hi):
-        r = slice(640 * o, 640 * (o + 1))
+        r = slice(576 * o, 576 * (o + 1))
         acc = nt(m.lt[sec, i, r, :], m.dsel[sec, core, lo:hi, :])
         acc = acc + nt(m.lt_in[sec, i, r, :], m.dsel_in[sec, lo:hi, :])
         return acc
@@ -297,8 +317,11 @@
     def widen(acc, width):
         return jnp.concatenate([acc, jnp.zeros((acc.shape[0], width - acc.shape[1]), F32)], axis=1)
 
+    def lower(acc):
+        return jnp.concatenate([acc[36:72], jnp.zeros((4, acc.shape[1]), F32)], axis=0).astype(BF)
+
     def blocks(acc):
-        return acc.reshape(4, 4, RB, acc.shape[1]).astype(BF)
+        return acc.reshape(4, 2, PB, acc.shape[1]).astype(BF)
 
     def grad_first(sec, n):
         dst = getattr(m, n + "_c")
@@ -352,13 +375,13 @@
             i = ring(o)
             up, dn, opp = lax.rem(i + 1, 4), lax.rem(i + 3, 4), lax.rem(i + 2, 4)
             one = [
-                remote(self.g.at[o * 4 + opp, 2 * k: 2 * k + 2], self.r1.at[o, k],
+                remote(self.g.at[o * 4 + opp, k], self.r1.at[o, k],
                        self.r1_s.at[o, k], self.r1_r.at[o, k], on_first(o, to))
                 for k, to in ((0, up), (1, dn))
             ]
             two = [
                 [
-                    remote(self.g.at[o * 4 + to, 2 * b: 2 * b + 2], self.r2.at[o, k, 2 * b: 2 * b + 2],
+                    remote(self.g.at[o * 4 + to, b], self.r2.at[o, k, b],
                            self.r2_s.at[o, k, b], self.r2_r.at[o, k, b], on_first(o, to))
                     for b in range(2)
                 ]
@@ -380,10 +403,9 @@
                 one, two, up, dn, i = self.first(o)
                 for side, chunk, b in ((0, up, 0), (1, dn, 1)):
                     one[side].wait_recv()
-                    for e in range(2):
-                        acc = self.g[o * 4 + chunk, 2 * b + e].astype(F32)
-                        acc = acc + self.r1[o, side, e].astype(F32)
-                        self.g[o * 4 + chunk, 2 * b + e] = acc.astype(BF)
+                    acc = self.g[o * 4 + chunk, b].astype(F32)
+                    acc = acc + self.r1[o, side].astype(F32)
+                    self.g[o * 4 + chunk, b] = acc.astype(BF)
                     two[side][b].start()
 
         def second_copies(self, o):
@@ -401,11 +423,12 @@
                 for side in two:
                     for c in side:
                         c.wait_recv()
-                for e in range(4):
+                for e in range(2):
                     acc = self.g[o * 4 + i, e].astype(F32)
                     acc = acc + self.r2[o, 0, e].astype(F32)
                     acc = acc + self.r2[o, 1, e].astype(F32)
-                    self.h[o, e] = acc.astype(BF)
+                    self.h[o, 2 * e] = acc[0:40].astype(BF)
+                    self.h[o, 2 * e + 1] = lower(acc)
                 for c in self.second_copies(o):
                     c.start()
 
@@ -468,10 +491,12 @@
                 c.wait_recv()
 
             def add(a, carry):
-                acc = self.c[zh, zl, a].astype(F32)
-                for d in range(3):
-                    acc = acc + self.ci[d, a].astype(F32)
-                self.cs[a] = acc.astype(BF)
+                for e in range(2):
+                    acc = self.c[zh, zl, a, e].astype(F32)
+                    for d in range(3):
+                        acc = acc + self.ci[d, a, e].astype(F32)
+                    self.cs[a, 2 * e] = acc[0:40].astype(BF)
+                    self.cs[a, 2 * e + 1] = lower(acc)
                 return carry
 
             lax.fori_loop(0, 4, add, 0)
@@ -510,47 +535,56 @@
 
     loads[0].wait()
     normalize(m.x, m.normed_s)
-    loads[4].wait()
-    qkv_heads(m.normed_s, m.wqs, m.hs_s)
     pl.semaphore_wait(barrier, NS + 2)
     a2a_start(0, ins[1], m.go)
     own = pltpu.make_async_copy(ins[1].at[me], m.go.at[me], m.load_sem.at[1])
     own.start()
-
-    def spatial_head(h, carry):
-        p = softmax(m.hs_s[h], m.hs_s[h + 8], None)
-        m.probs[h] = p
-        m.mh_s[h] = nt(m.hs_s[h + 16], p.astype(BF)).astype(BF)
-        return carry
-
-    lax.fori_loop(0, H, spatial_head, 0)
-    m.mixed[...] = heads(m.mh_s, range(H)).T.astype(BF)
+    loads[4].wait()
+    for i in (5, 2, 7, 3, 6):
+        loads[i].start()
+    qkv_heads(m.normed_s, m.wqs, m.hs_s)
+
     loads[2].wait()
     loads[5].wait()
-    for n in range(3):
-        c = slice(384 * n, 384 * (n + 1))
-        proj = nn(m.mixed[...], m.wos[:, c]).reshape(32, 8, 384)
-        keep = m.ks[:, :, c].astype(F32) * KEEP
-        m.y_out[:, :, c] = (m.x[:, :, c].astype(F32) + proj * keep).astype(BF)
-    a2a_start(1, m.y_out, m.y_in)
+    for half in range(2):
+        q_part, f_part = slice(128 * half, 128 * (half + 1)), slice(16 * half, 16 * (half + 1))
+
+        def spatial_head(h):
+            p = softmax(m.hs_s[h, :, q_part], m.hs_s[h + 8], None)
+            m.probs[h, q_part, :] = p
+            m.mh_s[h, :, q_part] = nt(m.hs_s[h + 16], p.astype(BF)).astype(BF)
+
+        some_heads(0, H, spatial_head)
+        part = jnp.concatenate([m.mh_s[h, :, q_part].astype(F32) for h in range(H)], axis=0)
+        m.mixed[q_part, :] = part.T.astype(BF)
+        for n in range(3):
+            c = slice(384 * n, 384 * (n + 1))
+            proj = nn(m.mixed[q_part, :], m.wos[:, c]).reshape(16, 8, 384)
+            keep = m.ks[f_part, :, c].astype(F32) * KEEP
+            m.y_out[f_part, :, c] = (m.x[f_part, :, c].astype(F32) + proj * keep).astype(BF)
+
+        def send_part(i, carry):
+            a2a_send(1, m.y_out, m.y_in, 16 * half + lax.rem(me + i, 16))
+            return carry
+
+        lax.fori_loop(0, 16, send_part, 0)
     m.y_in[me] = m.y_out[me]
 
     def perm_step(n, carry):
-        blocks = []
-        for k in (2 * n, 2 * n + 1):
-            o, a, b = k // 16, lax.rem(k // 4, 4), lax.rem(k, 4)
-            x = a * (1 - o) + b * o
-            y = b * (1 - o) + a * o
-            s = x * 8 + o * 4 + y
-            row = lax.broadcasted_iota(jnp.int32, (RB, D), 0)
-            col = lax.broadcasted_iota(jnp.int32, (RB, D), 1)
-            hit = (col == row + 36 * s) & (row < 36)
-            blocks.append(jnp.where(hit, 1.0, 0.0))
-        both = jnp.concatenate(blocks, axis=0).astype(BF)
-        m.perm[pl.ds(pl.multiple_of(n * 80, 80), 80), :] = both
+        o, a = n // 4, lax.rem(n, 4)
+        row = lax.broadcasted_iota(jnp.int32, (PB, D), 0)
+        col = lax.broadcasted_iota(jnp.int32, (PB, D), 1)
+        pairs = []
+        for b in (0, 2):
+            s0 = (a * (1 - o) + b * o) * 8 + o * 4 + b * (1 - o) + a * o
+            s1 = s0 + 8 * o + 1 - o
+            target = jnp.where(row < 36, row + 36 * s0, row + 36 * s1 - 36)
+            pairs.append(jnp.where(col == target, 1.0, 0.0))
+        both = jnp.concatenate(pairs, axis=0).astype(BF)
+        m.perm[pl.ds(pl.multiple_of(n * 144, 144), 144), :] = both
         return carry
 
-    lax.fori_loop(0, NS // 2, perm_step, 0)
+    lax.fori_loop(0, 8, perm_step, 0)
     gather_mixed(1, m.mh_s)
     core_copies(1)[3].start()
 
@@ -568,7 +602,7 @@
     loads[6].wait()
     qkv_heads(m.normed_t, m.wqt, m.hs_t)
 
-    def temporal_head(h, carry):
+    def temporal_head(h):
         i = lax.broadcasted_iota(jnp.int32, (T, T), 0)
         j = lax.broadcasted_iota(jnp.int32, (T, T), 1)
         mask = ((i - j) & 7) == 0
@@ -577,11 +611,13 @@
         p_low = p.astype(BF)
         m.mh_t[h] = nt(v, p_low).astype(BF)
         attention_backward(h, p, p_low, q, k, v)
-        return carry
-
-    lax.fori_loop(0, H, temporal_head, 0)
-    input_backward(m.y_in, m.go, m.d_out, m.wqt)
-    a2a_start(2, m.d_out, m.d_in)
+
+    some_heads(0, H, temporal_head)
+    def send_rows(r):
+        for j in range(4):
+            a2a_send(2, m.d_out, m.d_in, r * 4 + lax.rem(me + j, 4))
+
+    input_backward(m.y_in, m.go, m.d_out, m.wqt, send_rows)
     m.d_in[me] = m.d_out[me]
     gather_columns(0)
     gather_mixed(0, m.mh_t)
@@ -601,42 +637,42 @@
     d_proj_mix(m.d_in, m.ks, m.wos)
     transpose_rows(1, 1, m.dproj)
     core_copies(1)[1].start()
-    b_time.relay()
-
-    def spatial_back(h, carry):
+
+    def spatial_back(h):
         p = m.probs[h]
         attention_backward(h, p, p.astype(BF), m.hs_s[h], m.hs_s[h + 8], m.hs_s[h + 16])
-        return carry
-
-    lax.fori_loop(0, H, spatial_back, 0)
-    gather_columns(1)
-    core_copies(1)[2].start()
+
+    some_heads(0, H // 2, spatial_back)
+    b_time.relay()
     core_copies(1)[1].wait_recv()
     core_copies(1)[3].wait_recv()
     grad_out(1, "out")
     b_out.start()
+    some_heads(H // 2, H, spatial_back)
+    gather_columns(1)
+    core_copies(1)[2].start()
+    b_time.c_second()
+    b_time.second()
     core_copies(1)[0].wait_recv()
     core_copies(1)[2].wait_recv()
     grad_first(1, "space")
     b_space.c_start()
     grad_rest(1, "space")
     b_space.start()
-    b_time.second()
-    b_time.c_second()
     b_out.relay()
+    b_time.third()
     input_backward(m.x, m.d_in, m.dx, m.wqs)
     store = pltpu.make_async_copy(m.dx, dx_hbm, m.store_sem.at[0])
     store.start()
     b_space.relay()
-    b_space.c_second()
-    b_time.third()
     b_out.second()
-    b_space.second()
     first = b_time.c_end()
     rest = b_time.end()
     gqt[...] = jnp.concatenate([first[0:36], rest[0:36, 0:304]], axis=1)
     got[...] = rest[0:36, 304:448]
+    b_space.c_second()
     b_out.third()
+    b_space.second()
     b_space.third()
     first = b_space.c_end()
     gos[...] = b_out.end()[0:36, 0:144]

time: 90.6 us -> 88.2 us (0.974)
  Pallas kernels: 89.6 us -> 87.2 us
    pallas_call x1, Pallas kernels: 87.5 us -> 85.1 us  [shards(): pl.pallas_call(body, out_shape=(jax.ShapeDtypeStruct((32, 8, D), BF), jax...]
where the time goes in v4:
time: 88.2 us; the launch traced here: 88 us
  Pallas kernels  87.2 us (99%)
    pallas_call x1, Pallas kernels, shards(): pl.pallas_call(body, out_shape=(jax.ShapeDtypeStruct((32, 8, D), BF), jax...  85.1 us
    pallas_call x1, Pallas kernels, shards(): pl.pallas_call(hand_over, out_shape=tuple((jax.ShapeDtypeStruct(o.shape,...  2.08 us

profile of v4, /device:TPU:0, one launch (start us, length us, event | category | flops | bytes accessed | tf_op | source)
XLA Modules:
  0.0 88.0 jit_solution(11589353722219566667)
XLA Ops:
  0.6 85.1 %shard_map.119 = (bf16[32,8,1152]{2,1,0:T(8,128)(2,1)}, f32[36,432]{1,0:T(8,128)}, f32[36,144]{1,0:T(8,128)}, f32[36,432]{1,0:T(8,128)}, f32[36,144]{1,0:T(8,128)}) custom-call(bf16[32,8,1152]{2,1,0:T(8,128)(2,1)} %bitcast.15, bf16[32,8,1152]{2,1,0:T(8,128)(2,1)} %bitcast.16, s32[32,8,1152]{2,1,0:T(8,128)} %bitcast.13, s32[32,8,1152]{2,1,0:T(8,128)} %bitcast.14, ...), custom_call_target="tpu_custom_call" | custom-call | tf_op jit(solution)/shard_map/pallas_call | solution.py:714
  85.8 2.1 %shard_map.120 = (bf16[32,8,1152]{2,1,0:T(8,128)(2,1)}, f32[36,432]{1,0:T(8,128)}, f32[36,144]{1,0:T(8,128)}, f32[36,432]{1,0:T(8,128)}, f32[36,144]{1,0:T(8,128)}) custom-call(bf16[32,8,1152]{2,1,0:T(8,128)(2,1)} %get-tuple-element.15.refs_0_, f32[36,432]{1,0:T(8,128)} %get-tuple-element.16.refs_1_, f32[36,144]{1,0:T(8,128)} %get-tuple-element.17.refs_2_, ...), custom_call_target="tpu_custom_call" | custom-call | tf_op jit(solution)/shard_map/pallas_call | solution.py:740

commit v5 on v4

--- a/solution.py
+++ b/solution.py
@@ -74,20 +74,15 @@
     core_s=(2, 4),
     core_r=(2, 4),
 )
-BATCHES = dict(time=(896, 512, True), out=(384, 256, False), space=(640, 384, True))
-for _n, (_w, _z, _c) in BATCHES.items():
+BATCHES = dict(time=(896, True), out=(384, False), space=(640, True))
+for _n, (_w, _c) in BATCHES.items():
     SCRATCH.update({
         _n + "_g": ((8, 2, PB, _w), BF),
         _n + "_r1": ((2, 2, PB, _w), BF),
         _n + "_r2": ((2, 2, 2, PB, _w), BF),
-        _n + "_h": ((2, 4, RB, _w), BF),
-        _n + "_r3": ((2, 3, RB, _w), BF),
-        _n + "_z": ((2, 2, RB, _z), BF),
-        _n + "_r4": ((3, RB, _z), BF),
     })
     SEMS.update({
         _n + "_r1_s": (2, 2), _n + "_r1_r": (2, 2), _n + "_r2_s": (2, 2, 2), _n + "_r2_r": (2, 2, 2),
-        _n + "_r3_s": (2, 3), _n + "_r3_r": (2, 3), _n + "_r4_s": (3,), _n + "_r4_r": (3,),
     })
     if _c:
         SCRATCH.update({
@@ -95,7 +90,12 @@
             _n + "_ci": ((3, 4, 2, PB, 128), BF),
             _n + "_cs": ((4, 4, RB, 128), BF),
             _n + "_cj": ((15, RB, 128), BF),
+            _n + "_h": ((2, 4, RB, 896), BF),
+            _n + "_r3": ((2, 3, RB, 896), BF),
+            _n + "_z": ((2, 2, RB, 512), BF),
+            _n + "_r4": ((3, RB, 512), BF),
         })
+        SEMS.update({_n + "_r3_s": (2, 3), _n + "_r3_r": (2, 3), _n + "_r4_s": (3,), _n + "_r4_r": (3,)})
         SEMS.update({_n + "_ci_s": (3,), _n + "_ci_r": (3,), _n + "_cj_s": (15,), _n + "_cj_r": (15,)})
 
 
@@ -417,16 +417,26 @@
                 for d in (1, 2, 3)
             ]
 
+        def arrived(self, o):
+            one, two, up, dn, i = self.first(o)
+            for side in two:
+                for c in side:
+                    c.wait_recv()
+
+        def total(self, o, e):
+            acc = self.g[o * 4 + ring(o), e].astype(F32)
+            acc = acc + self.r2[o, 0, e].astype(F32)
+            return acc + self.r2[o, 1, e].astype(F32)
+
         def second(self):
             for o in range(2):
-                one, two, up, dn, i = self.first(o)
-                for side in two:
-                    for c in side:
-                        c.wait_recv()
+                self.arrived(o)
+                if self.n == "space":
+                    b_out.arrived(o)
                 for e in range(2):
-                    acc = self.g[o * 4 + i, e].astype(F32)
-                    acc = acc + self.r2[o, 0, e].astype(F32)
-                    acc = acc + self.r2[o, 1, e].astype(F32)
+                    acc = self.total(o, e)
+                    if self.n == "space":
+                        acc = jnp.concatenate([acc[:, :608], b_out.total(o, e)[:, :288]], axis=1)
                     self.h[o, 2 * e] = acc[0:40].astype(BF)
                     self.h[o, 2 * e + 1] = lower(acc)
                 for c in self.second_copies(o):
@@ -450,14 +460,11 @@
                 for d in range(3):
                     acc = acc + self.r3[o, d].astype(F32)
                 for z in range(2):
-                    if self.n == "out":
-                        v = acc[:, 144 * z: 144 * (z + 1)]
-                    else:
-                        v = acc[:, 304 * z: 304 * (z + 1)]
-                    if self.n == "time":
-                        low = 608 + 144 * z
-                        v = jnp.concatenate([v, acc[:, low: low + 144]], axis=1)
-                    self.z[o, z] = widen(v, BATCHES[self.n][1]).astype(BF)
+                    low = 608 + 144 * z
+                    v = jnp.concatenate(
+                        [acc[:, 304 * z: 304 * (z + 1)], acc[:, low: low + 144]], axis=1
+                    )
+                    self.z[o, z] = widen(v, 512).astype(BF)
             for c in self.z_copies():
                 c.start()
 
@@ -523,11 +530,11 @@
         def drain(self):
             for o in range(2):
                 one, two, up, dn, i = self.first(o)
-                for c in one + two[0] + two[1] + self.second_copies(o):
+                for c in one + two[0] + two[1]:
                     c.wait_send()
-            for c in self.z_copies():
-                c.wait_send()
             if self.c is not None:
+                for c in self.second_copies(0) + self.second_copies(1) + self.z_copies():
+                    c.wait_send()
                 for c in self.ci_copies() + self.cj_copies():
                     c.wait_send()
 
@@ -627,11 +634,11 @@
     core_copies(0)[0].start()
     for c in core_copies(0):
         c.wait_recv()
-    grad_first(0, "time")
-    b_time.c_start()
     grad_rest(0, "time")
     grad_out(0, "time")
     b_time.start()
+    grad_first(0, "time")
+    b_time.c_start()
 
     a2a_wait(2, m.d_out, m.d_in)
     d_proj_mix(m.d_in, m.ks, m.wos)
@@ -651,33 +658,31 @@
     some_heads(H // 2, H, spatial_back)
     gather_columns(1)
     core_copies(1)[2].start()
+    b_time.second()
     b_time.c_second()
-    b_time.second()
     core_copies(1)[0].wait_recv()
     core_copies(1)[2].wait_recv()
+    grad_rest(1, "space")
+    b_space.start()
     grad_first(1, "space")
     b_space.c_start()
-    grad_rest(1, "space")
-    b_space.start()
     b_out.relay()
     b_time.third()
     input_backward(m.x, m.d_in, m.dx, m.wqs)
     store = pltpu.make_async_copy(m.dx, dx_hbm, m.store_sem.at[0])
     store.start()
     b_space.relay()
-    b_out.second()
     first = b_time.c_end()
     rest = b_time.end()
     gqt[...] = jnp.concatenate([first[0:36], rest[0:36, 0:304]], axis=1)
     got[...] = rest[0:36, 304:448]
+    b_space.second()
     b_space.c_second()
-    b_out.third()
-    b_space.second()
     b_space.third()
     first = b_space.c_end()
-    gos[...] = b_out.end()[0:36, 0:144]
     rest = b_space.end()
     gqs[...] = jnp.concatenate([first[0:36], rest[0:36, 0:304]], axis=1)
+    gos[...] = rest[0:36, 304:448]
 
     a2a_drain(0, ins[1], m.go)
     a2a_drain(1, m.y_out, m.y_in)

time: 88.2 us -> 86.7 us (0.983)
  Pallas kernels: 87.2 us -> 85.8 us
    pallas_call x1, Pallas kernels: 85.1 us -> 83.7 us  [shards(): pl.pallas_call(body, out_shape=(jax.ShapeDtypeStruct((32, 8, D), BF), jax...]
where the time goes in v5:
time: 86.7 us; the launch traced here: 86.6 us
  Pallas kernels  85.8 us (99%)
    pallas_call x1, Pallas kernels, shards(): pl.pallas_call(body, out_shape=(jax.ShapeDtypeStruct((32, 8, D), BF), jax...  83.7 us
    pallas_call x1, Pallas kernels, shards(): pl.pallas_call(hand_over, out_shape=tuple((jax.ShapeDtypeStruct(o.shape,...  2.08 us

profile of v5, /device:TPU:0, one launch (start us, length us, event | category | flops | bytes accessed | tf_op | source)
XLA Modules:
  0.0 86.6 jit_solution(1239182330404418222)
XLA Ops:
  0.6 83.7 %shard_map.119 = (bf16[32,8,1152]{2,1,0:T(8,128)(2,1)}, f32[36,432]{1,0:T(8,128)}, f32[36,144]{1,0:T(8,128)}, f32[36,432]{1,0:T(8,128)}, f32[36,144]{1,0:T(8,128)}) custom-call(bf16[32,8,1152]{2,1,0:T(8,128)(2,1)} %bitcast.15, bf16[32,8,1152]{2,1,0:T(8,128)(2,1)} %bitcast.16, s32[32,8,1152]{2,1,0:T(8,128)} %bitcast.13, s32[32,8,1152]{2,1,0:T(8,128)} %bitcast.14, ...), custom_call_target="tpu_custom_call" | custom-call | tf_op jit(solution)/shard_map/pallas_call | solution.py:719
  84.3 2.1 %shard_map.120 = (bf16[32,8,1152]{2,1,0:T(8,128)(2,1)}, f32[36,432]{1,0:T(8,128)}, f32[36,144]{1,0:T(8,128)}, f32[36,432]{1,0:T(8,128)}, f32[36,144]{1,0:T(8,128)}) custom-call(bf16[32,8,1152]{2,1,0:T(8,128)(2,1)} %get-tuple-element.15.refs_0_, f32[36,432]{1,0:T(8,128)} %get-tuple-element.16.refs_1_, f32[36,144]{1,0:T(8,128)} %get-tuple-element.17.refs_2_, ...), custom_call_target="tpu_custom_call" | custom-call | tf_op jit(solution)/shard_map/pallas_call | solution.py:745

commit v6 on v5

--- a/solution.py
+++ b/solution.py
@@ -265,11 +265,14 @@
             hs = (2 * c, 2 * c + 1, 4 + 2 * c, 5 + 2 * c)
             m.dsel[sec, c, 864:1152] = heads(mh, hs).astype(BF)
 
-    def input_backward(src, dy, dst, wq, then=None):
+    def input_backward(src, dy, dst, wq, then=None, between=None):
         m.dqkv[:, 0:1152] = heads(m.dh, range(16)).T.astype(BF)
         m.dqkv[:, 1152:1728] = heads(m.dh, range(16, 24)).T.astype(BF)
         for n in range(3):
             m.dn[:, 384 * n: 384 * (n + 1)] = nn(m.dqkv[...], wq[:, 384 * n: 384 * (n + 1)])
+
+        if between is not None:
+            between()
 
         def fn(r, blk):
             zf = flat(src, blk)
@@ -668,10 +671,9 @@
     b_space.c_start()
     b_out.relay()
     b_time.third()
-    input_backward(m.x, m.d_in, m.dx, m.wqs)
+    input_backward(m.x, m.d_in, m.dx, m.wqs, between=b_space.relay)
     store = pltpu.make_async_copy(m.dx, dx_hbm, m.store_sem.at[0])
     store.start()
-    b_space.relay()
     first = b_time.c_end()
     rest = b_time.end()
     gqt[...] = jnp.concatenate([first[0:36], rest[0:36, 0:304]], axis=1)

time: 86.7 us -> 86.1 us (level)
  no operation moved by 1% of the time
where the time goes in v6:
time: 86.1 us; the launch traced here: 86 us
  Pallas kernels  85.2 us (99%)
    pallas_call x1, Pallas kernels, shards(): pl.pallas_call(body, out_shape=(jax.ShapeDtypeStruct((32, 8, D), BF), jax...  83.1 us
    pallas_call x1, Pallas kernels, shards(): pl.pallas_call(hand_over, out_shape=tuple((jax.ShapeDtypeStruct(o.shape,...  2.08 us

profile of v6, /device:TPU:0, one launch (start us, length us, event | category | flops | bytes accessed | tf_op | source)
XLA Modules:
  0.0 86.0 jit_solution(15091610274160559900)
XLA Ops:
  0.6 83.1 %shard_map.119 = (bf16[32,8,1152]{2,1,0:T(8,128)(2,1)}, f32[36,432]{1,0:T(8,128)}, f32[36,144]{1,0:T(8,128)}, f32[36,432]{1,0:T(8,128)}, f32[36,144]{1,0:T(8,128)}) custom-call(bf16[32,8,1152]{2,1,0:T(8,128)(2,1)} %bitcast.15, bf16[32,8,1152]{2,1,0:T(8,128)(2,1)} %bitcast.16, s32[32,8,1152]{2,1,0:T(8,128)} %bitcast.13, s32[32,8,1152]{2,1,0:T(8,128)} %bitcast.14, ...), custom_call_target="tpu_custom_call" | custom-call | tf_op jit(solution)/shard_map/pallas_call | solution.py:721
  83.8 2.1 %shard_map.120 = (bf16[32,8,1152]{2,1,0:T(8,128)(2,1)}, f32[36,432]{1,0:T(8,128)}, f32[36,144]{1,0:T(8,128)}, f32[36,432]{1,0:T(8,128)}, f32[36,144]{1,0:T(8,128)}) custom-call(bf16[32,8,1152]{2,1,0:T(8,128)(2,1)} %get-tuple-element.15.refs_0_, f32[36,432]{1,0:T(8,128)} %get-tuple-element.16.refs_1_, f32[36,144]{1,0:T(8,128)} %get-tuple-element.17.refs_2_, ...), custom_call_target="tpu_custom_call" | custom-call | tf_op jit(solution)/shard_map/pallas_call | solution.py:747
